TPU v7x, 32 devices: a whole 2x2x4 slice. The times are simulated.
32 devices in a mesh: group: 2 (over y), replica: 8 (over z, x), tensor: 2 (over core).
Axes of the slice: x: 2, y: 2, z: 4, core: 2. Of those that a mesh axis runs over, the one named last changes fastest.
Arguments:
- queries: bfloat16 [4096, 4096], P(('group', 'replica'), 'tensor'), parts along dimension 0, may hold values from -12 to 12
- keys: bfloat16 [4096, 512], P(('group', 'replica'), 'tensor'), parts along dimension 0, may hold values from -6 to 6
- values: bfloat16 [4096, 512], P(('group', 'replica'), 'tensor'), parts along dimension 0, may hold values from -6 to 6
- lengths: int32 [16], P('group'), parts along dimension 0, may hold values from 1 to 8, as said below
- slot_prompt: int32 [16, 2], P('group'), parts along dimension 0, may hold values from 0 to 7, as said below
- slot_span: int32 [16, 2], P('group'), parts along dimension 0, may hold values from 0 to 7
Outputs:
- attention: bfloat16 [16384, 4096], P(('group', 'replica'), 'tensor'), parts along dimension 0
- cache_keys: bfloat16 [16384, 512], P(('group', 'replica'), 'tensor'), parts along dimension 0
- cache_values: bfloat16 [16384, 512], P(('group', 'replica'), 'tensor'), parts along dimension 0
There are 2 independent parts, one for each index of `group`. A program takes and returns all parts, laid end to end along the dimension named above; each array names one. Nothing has to cross between parts.
Inputs may be any that keep to these rules, and one draw needn't show every extreme that they name: The lengths sum to 16, and some prompt has exactly 8 spans. Every slot holds one span: each pair of a prompt p and a span m < lengths[p] is named by exactly one slot through slot_prompt and slot_span, and no other pair is named. Span m < min(lengths[p], 2) of prompt p sits in slot m of replica p.
All inputs are finite; a program needn't handle non-finite values.
Results may differ from a plain program's by a relative error of at most 0.0047.
Values may be sent and summed in bfloat16 or wider, within the bound.
No kernel may reach another device: no remote copies, remote signals or barrier semaphores. Data moves between devices by JAX's collectives and lax.ppermute only.
A program may use at most 128 MiB of HBM per device.

v0:
```python
import functools
import math

import jax
import jax.numpy as jnp
from jax import lax
from jax.experimental import pallas as pl
from jax.experimental.pallas import tpu as pltpu
from jax.sharding import PartitionSpec as P

HDIM = 128
SPAN = 128
SLOTS = 2
MAXC = 8
BLOCK = 4
PART = 2
LOG2E = 1.0 / math.log(2.0)
VMEM_BYTES = 40 * 1024 * 1024
MOST_VMEM_BYTES = 60 * 1024 * 1024
LEAST_SUM, MOST_SUM = 1e-20, 1e30
ANY = pl.BlockSpec(memory_space=pl.ANY)
SMEM = pl.BlockSpec(memory_space=pltpu.SMEM)
VMEM = pl.BlockSpec(memory_space=pltpu.VMEM)


def cost_of(us):
    return pl.CostEstimate(flops=int(us * 1.15e9), bytes_accessed=0, transcendentals=0)


def column_ring(replicas):
    return list(range(0, replicas, 2)) + list(range(replicas - 1, 0, -2))


def pass_on(fetches, stores):
    for copy in fetches:
        copy.start()
    for copy in fetches:
        copy.wait()
    for copy in stores:
        copy.start()
    for copy in stores:
        copy.wait()


def pack_kv_kernel(k_ref, v_ref, o_ref, buf, sems):
    pass_on(
        [
            pltpu.make_async_copy(k_ref.at[SPAN:], buf.at[:SPAN], sems.at[0]),
            pltpu.make_async_copy(v_ref.at[SPAN:], buf.at[SPAN:], sems.at[1]),
        ],
        [pltpu.make_async_copy(buf, o_ref, sems.at[2])],
    )


def pack_kv(keys, values):
    shape = (2 * SPAN, keys.shape[1])
    return pl.pallas_call(
        pack_kv_kernel,
        out_shape=jax.ShapeDtypeStruct(shape, keys.dtype),
        in_specs=[ANY] * 2,
        out_specs=ANY,
        scratch_shapes=[pltpu.VMEM(shape, keys.dtype), pltpu.SemaphoreType.DMA((3,))],
        compiler_params=pltpu.CompilerParams(vmem_limit_bytes=MOST_VMEM_BYTES),
        cost_estimate=cost_of(1.7),
    )(keys, values)


def pack_q_kernel(q_ref, o_top, o_bottom, buf, sems):
    half = SPAN // 2
    pass_on(
        [
            pltpu.make_async_copy(q_ref.at[SPAN : SPAN + half], buf.at[:half], sems.at[0]),
            pltpu.make_async_copy(q_ref.at[SPAN + half :], buf.at[half:], sems.at[1]),
        ],
        [
            pltpu.make_async_copy(buf.at[:half], o_top, sems.at[2]),
            pltpu.make_async_copy(buf.at[half:], o_bottom, sems.at[3]),
        ],
    )


def pack_q(queries):
    width = queries.shape[1]
    half = jax.ShapeDtypeStruct((SPAN // 2, width), queries.dtype)
    return pl.pallas_call(
        pack_q_kernel,
        out_shape=(half, half),
        in_specs=[ANY],
        out_specs=(ANY, ANY),
        scratch_shapes=[
            pltpu.VMEM((SPAN, width), queries.dtype),
            pltpu.SemaphoreType.DMA((4,)),
        ],
        compiler_params=pltpu.CompilerParams(vmem_limit_bytes=MOST_VMEM_BYTES),
        cost_estimate=cost_of(1.7),
    )(queries)


def places(lengths, slot_prompt, slot_span):
    replicas = lengths.shape[0]
    mine = lax.axis_index("replica")
    ring = jnp.arange(replicas, dtype=jnp.int32)
    place = jnp.where(mine % 2 == 0, mine // 2, replicas - 1 - mine // 2)
    at = (place + replicas - ring) % replicas
    other = jnp.where(at < replicas // 2, 2 * at, 2 * (replicas - at) - 1)
    chosen = other[:, None] == ring[None, :]
    wanted = chosen & (slot_prompt[None, :, 1] == mine) & (ring[:, None] > 0)
    spans = jnp.where(wanted, slot_span[None, :, 1] + 1, 0)
    whole = jnp.where(chosen & (ring[:, None] == 0), lengths[None, :] + 1, 0)
    return jnp.sum(spans + whole, axis=1) - 1


def widen(v_ref, wide_ref):
    for at in range(0, v_ref.shape[-1], HDIM):
        wide_ref[:, 2 * at : 2 * at + HDIM] = v_ref[:, at : at + HDIM]
        wide_ref[:, 2 * at + HDIM : 2 * at + 2 * HDIM] = jnp.ones(
            (v_ref.shape[0], HDIM), v_ref.dtype
        )


def stack(q_refs, stacked):
    kv_heads, rows, _ = stacked.shape
    group = rows // SPAN
    for shared in range(kv_heads):
        for h in range(group):
            at = (shared * group + h) * HDIM
            row = h * SPAN
            for q_ref in q_refs:
                many = q_ref.shape[0]
                stacked[shared, row : row + many, :] = q_ref[:, at : at + HDIM]
                row += many


def attend_span(span, stacked, k_ref, wide_ref, mixed):
    kv_heads, rows, _ = stacked.shape
    heads = range(kv_heads)
    scale = LOG2E / math.sqrt(HDIM)
    blocks = span // BLOCK
    edge = span % PART * SPAN

    def keys_of(block, spans):
        return pl.ds(pl.multiple_of(block * BLOCK * SPAN, BLOCK * SPAN), spans * SPAN)

    def scores(shared, block, spans, masked):
        found = lax.dot_general(
            stacked[shared],
            k_ref[keys_of(block, spans), shared * HDIM : (shared + 1) * HDIM],
            (((1,), (1,)), ((), ())),
            preferred_element_type=jnp.float32,
        )
        if masked:
            seen = (spans - PART) * SPAN
            row = lax.broadcasted_iota(jnp.int32, (rows, PART * SPAN), 0) % SPAN
            column = lax.broadcasted_iota(jnp.int32, (rows, PART * SPAN), 1)
            last = jnp.where(column <= row + edge, found[:, seen:], -jnp.inf)
            found = jnp.concatenate([found[:, :seen], last], axis=1) if seen else last
        return found

    def products(shared, block, spans, found):
        return jnp.dot(
            jnp.exp2(found * scale).astype(jnp.bfloat16),
            wide_ref[keys_of(block, spans), 2 * shared * HDIM : 2 * (shared + 1) * HDIM],
            preferred_element_type=jnp.float32,
        )

    most = k_ref.shape[0] // SPAN
    for spans in range(PART, min(BLOCK, most) + 1, PART):

        @pl.when(span % BLOCK // PART == spans // PART - 1)
        def _(spans=spans):
            found = [scores(shared, blocks, spans, True) for shared in heads]
            for shared in heads:
                mixed[shared] = products(shared, blocks, spans, found[shared])

    def add(block, carry):
        found = [scores(shared, block, BLOCK, False) for shared in heads]
        for shared in heads:
            mixed[shared] += products(shared, block, BLOCK, found[shared])
        return carry

    if most > BLOCK:
        lax.fori_loop(0, blocks, add, 0)


def attend_span_shifted(span, stacked, k_ref, wide_ref, mixed, top):
    kv_heads, rows, _ = stacked.shape
    scale = LOG2E / math.sqrt(HDIM)

    def one_head(shared, carry):
        def scores(block):
            found = lax.dot_general(
                stacked[shared],
                k_ref[rows_of(block), pl.ds(pl.multiple_of(shared * HDIM, HDIM), HDIM)],
                (((1,), (1,)), ((), ())),
                preferred_element_type=jnp.float32,
            )
            row = lax.broadcasted_iota(jnp.int32, (rows, SPAN), 0) % SPAN
            column = lax.broadcasted_iota(jnp.int32, (rows, SPAN), 1)
            return jnp.where(column <= row + (span - block) * SPAN, found, -jnp.inf)

        def look(block, carry):
            top[...] = jnp.maximum(top[...], scores(block))
            return carry

        def add(block, carry):
            weights = jnp.exp2((scores(block) - top[...]) * scale).astype(jnp.bfloat16)
            mixed[shared] += jnp.dot(
                weights,
                wide_ref[
                    rows_of(block), pl.ds(pl.multiple_of(2 * shared * HDIM, 2 * HDIM), 2 * HDIM)
                ],
                preferred_element_type=jnp.float32,
            )
            return carry

        top[...] = jnp.full_like(top, -jnp.inf)
        lax.fori_loop(0, span + 1, look, 0)
        top[...] = jnp.broadcast_to(jnp.max(top[...], axis=1, keepdims=True), top.shape)
        mixed[shared] = jnp.zeros(mixed.shape[1:], mixed.dtype)
        lax.fori_loop(0, span + 1, add, 0)
        return carry

    lax.fori_loop(0, kv_heads, one_head, 0)


def finish(mixed, o_ref, bounds):
    kv_heads, rows, _ = mixed.shape
    for shared in range(kv_heads):
        total = mixed[shared, :, HDIM:]
        inverse = pl.reciprocal(total, approx=True)
        inverse = inverse * (2.0 - total * inverse)
        result = (mixed[shared, :, :HDIM] * inverse).astype(o_ref.dtype)
        for h in range(rows // SPAN):
            at = (shared * rows // SPAN + h) * HDIM
            o_ref[:, at : at + HDIM] = result[h * SPAN : (h + 1) * SPAN, :]
        total = total.reshape(-1, 8, HDIM)
        bounds[0] = jnp.minimum(bounds[0], jnp.min(total, axis=0))
        bounds[1] = jnp.maximum(bounds[1], jnp.max(total, axis=0))


def twice_if_needed(work, drain, bounds):
    bounds[...] = jnp.ones_like(bounds)
    work(False)
    safe = (jnp.min(bounds[0]) > LEAST_SUM) & (jnp.max(bounds[1]) < MOST_SUM)
    drain()

    @pl.when(jnp.logical_not(safe))
    def _():
        work(True)
        drain()


def work_space(count, width, key_width):
    kv_heads = key_width // HDIM
    rows = width // key_width * SPAN
    return [
        pltpu.VMEM((count, kv_heads, rows, HDIM), jnp.bfloat16),
        pltpu.VMEM((kv_heads, rows, 2 * HDIM), jnp.float32),
        pltpu.VMEM((rows, HDIM), jnp.float32),
        pltpu.VMEM((2, 8, HDIM), jnp.float32),
    ]


def rows_of(span):
    return pl.ds(pl.multiple_of(span * SPAN, SPAN), SPAN)


def attend_blocks(dests, q_parts, k_ref, wide_ref, out_buf, store, stacked, mixed, top, bounds):
    count = len(dests)
    for j in range(count):

        @pl.when(dests[j] >= 0)
        def _(j=j):
            stack(q_parts[j], stacked.at[j])

    def work(shifted):
        def one(j, carry):
            dest = dests[0]
            for n in range(1, count):
                dest = jnp.where(j == n, dests[n], dest)

            @pl.when(dest >= 0)
            def _():
                if shifted:
                    attend_span_shifted(dest, stacked.at[j], k_ref, wide_ref, mixed, top)
                else:
                    attend_span(dest, stacked.at[j], k_ref, wide_ref, mixed)
                finish(mixed, out_buf.at[j], bounds)
                if store is not None:
                    store(j, dest).start()

            return carry

        lax.fori_loop(0, count, one, 0)

    def drain():
        if store is not None:
            for j in range(count):
                pl.when(dests[j] >= 0)(store(j, jnp.maximum(dests[j], 0)).wait)

    twice_if_needed(work, drain, bounds)


def stores(buf, o_ref, sems):
    return lambda j, span: pltpu.make_async_copy(buf.at[j], o_ref.at[rows_of(span)], sems.at[j])


def local_kernel(length_ref, q_hbm, k_hbm, v_hbm, o_ref, q_ref, k_ref, v_ref, wide, zeros, sems, out_buf, out_sems, *work):
    live = length_ref[lax.axis_index("replica")]
    fetches = [
        pltpu.make_async_copy(k_hbm, k_ref, sems.at[0]),
        pltpu.make_async_copy(v_hbm, v_ref, sems.at[MAXC]),
        pltpu.make_async_copy(q_hbm, q_ref, sems.at[MAXC + 1]),
    ]
    for copy in fetches:
        copy.start()
    zeros[...] = jnp.zeros_like(zeros)

    def clear(span):
        return pltpu.make_async_copy(zeros, o_ref.at[rows_of(span)], sems.at[span])

    for span in range(1, MAXC):
        pl.when(span >= live)(clear(span).start)
    for copy in fetches:
        copy.wait()
    widen(v_ref, wide)
    attend_blocks(
        [jnp.int32(0), jnp.where(live > 1, 1, -1)],
        [(q_ref.at[:SPAN],), (q_ref.at[SPAN:],)],
        k_ref,
        wide,
        out_buf,
        stores(out_buf, o_ref, out_sems),
        *work,
    )
    for span in range(1, MAXC):
        pl.when(span >= live)(clear(span).wait)


def attend_local(lengths, queries, keys, values):
    width, key_width = queries.shape[1], keys.shape[1]
    return pl.pallas_call(
        local_kernel,
        out_shape=jax.ShapeDtypeStruct((MAXC * SPAN, width), queries.dtype),
        in_specs=[SMEM, ANY, ANY, ANY],
        out_specs=ANY,
        scratch_shapes=[
            pltpu.VMEM(queries.shape, queries.dtype),
            pltpu.VMEM(keys.shape, keys.dtype),
            pltpu.VMEM(values.shape, values.dtype),
            pltpu.VMEM((SLOTS * SPAN, 2 * key_width), keys.dtype),
            pltpu.VMEM((SPAN, width), queries.dtype),
            pltpu.SemaphoreType.DMA((MAXC + 2,)),
            pltpu.VMEM((SLOTS, SPAN, width), queries.dtype),
            pltpu.SemaphoreType.DMA((SLOTS,)),
            *work_space(SLOTS, width, key_width),
        ],
        compiler_params=pltpu.CompilerParams(vmem_limit_bytes=MOST_VMEM_BYTES),
        cost_estimate=cost_of(5),
    )(lengths, queries, keys, values)


def parts_of(refs, pieces):
    return [refs[sum(pieces[:j]) : sum(pieces[: j + 1])] for j in range(len(pieces))]


def any_of(dests):
    return functools.reduce(jnp.maximum, dests) >= 0


def first_kernel(kv_offsets, offsets, pieces, meta_ref, own_k, own_v, *refs):
    parts = sum(pieces)
    blocks, refs = refs[: len(kv_offsets)], refs[len(kv_offsets) :]
    q_refs, refs = refs[:parts], refs[parts:]
    o_k, o_v, k_buf, wide, out_buf, v_buf, in_sems, out_sems, *work = refs
    live = meta_ref[0]

    def fetches():
        yield None, own_k.at[:SPAN], k_buf.at[rows_of(0)]
        yield None, own_v.at[:SPAN], v_buf.at[rows_of(0)]
        yield live > 1, own_k.at[SPAN:], k_buf.at[rows_of(1)]
        yield live > 1, own_v.at[SPAN:], v_buf.at[rows_of(1)]

    def each(act):
        for n, (needed, here, there) in enumerate(fetches()):
            copy = getattr(pltpu.make_async_copy(here, there, in_sems.at[n]), act)
            if needed is None:
                copy()
            else:
                pl.when(needed)(copy)

    each("start")
    for span in range(1, MAXC):

        @pl.when(span >= live)
        def _(span=span):
            k_buf[rows_of(span), :] = jnp.zeros((SPAN, k_buf.shape[1]), k_buf.dtype)
            v_buf[rows_of(span), :] = jnp.zeros((SPAN, v_buf.shape[1]), v_buf.dtype)

    for block, offset in zip(blocks, kv_offsets, strict=True):
        dest = meta_ref[offset]

        @pl.when(dest >= 0)
        def _(block=block, dest=dest):
            k_buf[rows_of(dest), :] = block[:SPAN, :]
            v_buf[rows_of(dest), :] = block[SPAN:, :]

    each("wait")
    copy_k = pltpu.make_async_copy(k_buf, o_k, out_sems.at[0])
    copy_v = pltpu.make_async_copy(v_buf, o_v, out_sems.at[1])
    copy_k.start()
    copy_v.start()
    dests = [meta_ref[offset] for offset in offsets]

    @pl.when(live > 1)
    def _():
        widen(v_buf, wide)

    @pl.when(any_of(dests))
    def _():
        attend_blocks(dests, parts_of(q_refs, pieces), k_buf, wide, out_buf, None, *work)

    copy_k.wait()
    copy_v.wait()


def attend_first(meta, keys, values, kv_offsets, kv_blocks, offsets, blocks):
    rows, key_width = MAXC * SPAN, keys.shape[1]
    pieces = [len(block) for block in blocks]
    count, width = len(pieces), blocks[0][0].shape[1]
    out = jax.ShapeDtypeStruct((rows, key_width), keys.dtype)
    return pl.pallas_call(
        lambda *refs: first_kernel(kv_offsets, offsets, pieces, *refs),
        out_shape=(
            out,
            out,
            out,
            jax.ShapeDtypeStruct((rows, 2 * key_width), keys.dtype),
            jax.ShapeDtypeStruct((count, SPAN, width), keys.dtype),
        ),
        in_specs=[SMEM, ANY, ANY] + [VMEM] * (len(kv_blocks) + sum(pieces)),
        out_specs=(ANY, ANY, VMEM, VMEM, VMEM),
        scratch_shapes=[
            pltpu.VMEM((rows, key_width), keys.dtype),
            pltpu.SemaphoreType.DMA((4,)),
            pltpu.SemaphoreType.DMA((2,)),
            *work_space(count, width, key_width),
        ],
        compiler_params=pltpu.CompilerParams(vmem_limit_bytes=VMEM_BYTES),
        cost_estimate=cost_of(1 * (2 + 2.5 * count)),
    )(meta, keys, values, *kv_blocks, *[part for block in blocks for part in block])


def later_kernel(offsets, pieces, meta_ref, *refs):
    parts = sum(pieces)
    q_refs, (k_ref, wide_ref, out_buf, *work) = refs[:parts], refs[parts:]
    dests = [meta_ref[offset] for offset in offsets]

    @pl.when(any_of(dests))
    def _():
        attend_blocks(dests, parts_of(q_refs, pieces), k_ref, wide_ref, out_buf, None, *work)


def attend_later(meta, offsets, blocks, ordered_keys, wide_values):
    pieces = [len(block) for block in blocks]
    count, width = len(pieces), blocks[0][0].shape[1]
    return pl.pallas_call(
        lambda *refs: later_kernel(offsets, pieces, *refs),
        out_shape=jax.ShapeDtypeStruct((count, SPAN, width), ordered_keys.dtype),
        in_specs=[SMEM] + [VMEM] * (sum(pieces) + 2),
        out_specs=VMEM,
        scratch_shapes=work_space(count, width, ordered_keys.shape[1]),
        compiler_params=pltpu.CompilerParams(vmem_limit_bytes=VMEM_BYTES),
        cost_estimate=cost_of(1 * (1 + 2.5 * count)),
    )(meta, *[part for block in blocks for part in block], ordered_keys, wide_values)


def last_kernel(before, offsets, pieces, meta_ref, *refs):
    parts = sum(pieces)
    results, refs = refs[: len(before)], refs[len(before) :]
    q_refs, (k_ref, wide_ref, _, o_ref, out_buf, sems, out_sems, *work) = refs[:parts], refs[parts:]
    earlier = [
        (meta_ref[offset], result, j, n)
        for n, (result, its_offsets) in enumerate(zip(results, before, strict=True))
        for j, offset in enumerate(its_offsets)
    ]

    def each(act):
        for dest, result, j, n in earlier:
            copy = pltpu.make_async_copy(
                result.at[j], o_ref.at[rows_of(jnp.maximum(dest, 0))], sems.at[n, j]
            )
            pl.when(dest >= 0)(getattr(copy, act))

    each("start")
    dests = [meta_ref[offset] for offset in offsets]

    @pl.when(any_of(dests))
    def _():
        attend_blocks(
            dests,
            parts_of(q_refs, pieces),
            k_ref,
            wide_ref,
            out_buf,
            stores(out_buf, o_ref, out_sems),
            *work,
        )

    each("wait")


def attend_last(meta, before, results, offsets, blocks, ordered_keys, wide_values, attention):
    pieces = [len(block) for block in blocks]
    count, parts = len(pieces), sum(pieces)
    width = attention.shape[1]
    most = max(len(its_offsets) for its_offsets in before)
    return pl.pallas_call(
        lambda *refs: last_kernel(before, offsets, pieces, *refs),
        out_shape=jax.ShapeDtypeStruct(attention.shape, attention.dtype),
        in_specs=[SMEM] + [VMEM] * (len(results) + parts + 2) + [ANY],
        out_specs=ANY,
        input_output_aliases={len(results) + parts + 3: 0},
        scratch_shapes=[
            pltpu.VMEM((count, SPAN, width), attention.dtype),
            pltpu.SemaphoreType.DMA((len(before), most)),
            pltpu.SemaphoreType.DMA((count,)),
            *work_space(count, width, ordered_keys.shape[1]),
        ],
        compiler_params=pltpu.CompilerParams(vmem_limit_bytes=VMEM_BYTES),
        cost_estimate=cost_of(4),
    )(
        meta,
        *results,
        *[part for block in blocks for part in block],
        ordered_keys,
        wide_values,
        attention,
    )


def gathered_kernel(meta_ref, first_ref, later_ref, k_ref, v_ref, o_ref, wide, stacked, mixed, top, bounds):
    at = pl.program_id(1)
    live = meta_ref[0]
    widen(v_ref, wide)

    @pl.when(at == 0)
    def _():
        stack((first_ref,), stacked.at[0])

    @pl.when(at > 0)
    def _():
        stack((later_ref.at[0],), stacked.at[0])

    def work(shifted):
        if shifted:
            attend_span_shifted(at, stacked.at[0], k_ref, wide, mixed, top)
        else:
            attend_span(at, stacked.at[0], k_ref, wide, mixed)
        finish(mixed, o_ref, bounds)

    @pl.when(at < live)
    def _():
        twice_if_needed(work, lambda: None, bounds)

    @pl.when(at >= live)
    def _():
        o_ref[...] = jnp.zeros_like(o_ref)


def attend_gathered(live, source, first, later, cache_keys, cache_values):
    home_rows, key_width = cache_keys.shape
    width = first.shape[1]
    groups = key_width // HDIM
    part = width // groups
    meta = jnp.concatenate([live.reshape(1), source]).astype(jnp.int32)
    return pl.pallas_call(
        gathered_kernel,
        out_shape=jax.ShapeDtypeStruct((home_rows, width), first.dtype),
        grid_spec=pltpu.PrefetchScalarGridSpec(
            num_scalar_prefetch=1,
            grid=(groups, MAXC),
            in_specs=[
                pl.BlockSpec((SPAN, part), lambda g, m, meta: (0, g)),
                pl.BlockSpec((1, SPAN, part), lambda g, m, meta: (meta[1 + m], 0, g)),
                pl.BlockSpec((home_rows, HDIM), lambda g, m, meta: (0, g)),
                pl.BlockSpec((home_rows, HDIM), lambda g, m, meta: (0, g)),
            ],
            out_specs=pl.BlockSpec((SPAN, part), lambda g, m, meta: (m, g)),
            scratch_shapes=[
                pltpu.VMEM((home_rows, 2 * HDIM), cache_keys.dtype),
                *work_space(1, part, HDIM),
            ],
        ),
        compiler_params=pltpu.CompilerParams(vmem_limit_bytes=VMEM_BYTES),
    )(meta, first, later, cache_keys, cache_values)


def gather_all(queries, keys, values, lengths, slot_prompt, slot_span):
    mine = lax.axis_index("replica")
    home_rows, key_width = MAXC * SPAN, keys.shape[1]
    live = lengths[mine]
    spans = jnp.arange(MAXC, dtype=jnp.int32)
    matches = (slot_prompt[None, :, 1] == mine) & (slot_span[None, :, 1] == spans[:, None])
    here = jnp.any(matches, axis=1)
    source = jnp.argmax(matches, axis=1).astype(jnp.int32)
    slots_k = lax.all_gather(keys[SPAN:], "replica")
    slots_v = lax.all_gather(values[SPAN:], "replica")
    slots_q = lax.all_gather(queries[SPAN:], "replica")

    def in_order(first, slots):
        picked = jnp.take(slots, source, axis=0)
        kept = jnp.where(here[:, None, None], picked, jnp.zeros((), slots.dtype))
        return jnp.concatenate([first, kept[1:].reshape(home_rows - SPAN, key_width)], axis=0)

    cache_keys = in_order(keys[:SPAN], slots_k)
    cache_values = in_order(values[:SPAN], slots_v)
    attention = attend_gathered(live, source, queries[:SPAN], slots_q, cache_keys, cache_values)
    return (attention, cache_keys, cache_values)


def per_device(queries, keys, values, lengths, slot_prompt, slot_span):
    replicas = lax.axis_size("replica")
    if replicas != 8:
        return gather_all(queries, keys, values, lengths, slot_prompt, slot_span)
    ring = column_ring(replicas)
    farthest = replicas // 2

    def after(block, *others):
        return lax.optimization_barrier((block, others))[0]

    def joined(both):
        return list(lax.optimization_barrier(tuple(both)))

    def shift(block, step):
        pairs = [(r, ring[(n + step) % replicas]) for n, r in enumerate(ring)]
        return lax.ppermute(block, "replica", pairs)

    def go_on(both):
        return [shift(both[0], 1), shift(both[1], -1)]

    own_kv = pack_kv(keys, values)
    kv = [[own_kv, own_kv]]
    kv.append(go_on(kv[0]))
    own_top, own_bottom = pack_q(after(queries, own_kv))
    top, bottom = [[own_top, own_top]], [[own_bottom, own_bottom]]
    top.append(joined(go_on(top[0])))
    kv[1] = joined(kv[1])
    kv.append(joined(go_on(kv[1])))
    attention = attend_local(lengths, after(queries, kv[1]), keys, values)
    bottom.append(joined(go_on([after(block, top[1]) for block in bottom[0]])))
    kv.append(joined(go_on([after(block, attention) for block in kv[2]])))
    top.append(joined(go_on([after(block, kv[3]) for block in top[1]])))
    kv.append([shift(kv[3][0], 1)])
    bottom.append(joined(go_on([after(block, kv[3]) for block in bottom[1]])))
    meta = places(lengths, slot_prompt, slot_span)
    offsets = [[n, replicas - n] for n in range(1, farthest)]

    def blocks(n):
        return list(zip(top[n], bottom[n], strict=True))

    cache_keys, cache_values, ordered_keys, wide_values, result = attend_first(
        meta, keys, values, sum(offsets, []) + [farthest], sum(kv[1:], []), offsets[0], blocks(1)
    )
    results = [result]
    top.append(joined(go_on(top[2])))
    bottom.append(joined(go_on([after(block, results[0]) for block in bottom[2]])))
    results.append(attend_later(meta, offsets[1], blocks(2), ordered_keys, wide_values))
    last = (
        shift(after(top[3][0], results[1]), 1),
        shift(after(bottom[3][1], results[1]), -1),
    )
    results.append(attend_later(meta, offsets[2], blocks(3), ordered_keys, wide_values))
    attention = attend_last(
        meta, offsets, results, [farthest], [last], ordered_keys, wide_values, attention
    )
    return (attention, cache_keys, cache_values)


def solution(mesh):
    in_specs = (
        P(("group", "replica"), "tensor"),
        P(("group", "replica"), "tensor"),
        P(("group", "replica"), "tensor"),
        P("group"),
        P("group", None),
        P("group", None),
    )
    out_specs = (
        P(("group", "replica"), "tensor"),
        P(("group", "replica"), "tensor"),
        P(("group", "replica"), "tensor"),
    )
    return jax.shard_map(
        per_device, mesh=mesh, in_specs=in_specs, out_specs=out_specs, check_vma=False
    )
```

profile of v0, /device:TPU:2, one launch (start us, length us, event | category | flops | bytes accessed | tf_op | source)
XLA Modules:
  0.0 123.3 jit_solution(2337386317639714508)
XLA Ops:
  0.6 1.6 %shard_map.85 = bf16[256,256]{1,0:T(8,128)(2,1)} custom-call(bf16[256,256]{1,0:T(8,128)(2,1)} %refs_1_.1, bf16[256,256]{1,0:T(8,128)(2,1)} %refs_2_.1), custom_call_target="tpu_custom_call" | custom-call | flops 1955000064 | tf_op jit(solution)/shard_map/pallas_call | solution.py:57
  2.2 0.0 copy-start.4
  2.2 0.0 copy-start.5
  2.2 0.0 copy-start.2
  2.2 1.6 %collective-permute-start.1 = (bf16[256,256]{1,0:T(8,128)(2,1)}, bf16[256,256]{1,0:T(8,128)(2,1)S(1)}, u32[]{:S(2)}, u32[]{:S(2)}) collective-permute-start(bf16[256,256]{1,0:T(8,128)(2,1)} %shard_map.85), channel_id=1, source_target_pairs={{0,2},{4,0},{8,4},{12,8},{14,12},{10,14},{6,10},{2,6},{1,3},{5,1},... | collective-permute-start | bytes 393224 | tf_op jit(solution)/shard_map/ppermute | solution.py:637
  3.9 0.4 collective-permute-start
  4.3 1.8 %shard_map.87 = (bf16[64,2048]{1,0:T(8,128)(2,1)}, bf16[64,2048]{1,0:T(8,128)(2,1)}) custom-call(bf16[256,2048]{1,0:T(8,128)(2,1)} %q_ref), custom_call_target="tpu_custom_call" | custom-call | flops 1955000064 | tf_op jit(solution)/shard_map/pallas_call | solution.py:85
  6.2 1.6 %collective-permute-start.8 = (bf16[64,2048]{1,0:T(8,128)(2,1)}, bf16[64,2048]{1,0:T(8,128)(2,1)S(1)}, u32[]{:S(2)}, u32[]{:S(2)}) collective-permute-start(bf16[64,2048]{1,0:T(8,128)(2,1)} %get-tuple-element.51), channel_id=1, source_target_pairs={{0,2},{4,0},{8,4},{12,8},{14,12},{10,14},{6,10},{2,6},{1,3},{5,1},... | collective-permute-start | bytes 786440 | tf_op jit(solution)/shard_map/ppermute | solution.py:637
  7.8 0.4 collective-permute-start.7
  8.2 0.0 copy-done.4
  8.3 0.0 copy-done.5
  8.3 0.0 copy-done.2
  8.3 0.0 copy-start.3
  8.3 0.0 copy-start
  8.3 0.0 copy-start.1
  8.4 0.0 collective-permute-done.1.refs_4_
  8.4 0.7 collective-permute-done.refs_3_
  9.0 0.4 collective-permute-start.2
  9.5 1.6 %collective-permute-start.3 = (bf16[256,256]{1,0:T(8,128)(2,1)S(1)}, bf16[256,256]{1,0:T(8,128)(2,1)S(1)}, u32[]{:S(2)}, u32[]{:S(2)}) collective-permute-start(bf16[256,256]{1,0:T(8,128)(2,1)S(1)} %collective-permute-done.1.refs_4_), channel_id=1, source_target_pairs={{0,2},{4,0},{8,4},{12,8},{14,12},{10,14},{6,10},{2,6},{1,3},{5,1},... | collective-permute-start | bytes 393224 | tf_op jit(solution)/shard_map/ppermute | solution.py:637
  11.1 13.0 %shard_map.86.refs_8_ = bf16[1024,2048]{1,0:T(8,128)(2,1)} custom-call(s32[8]{0:T(128)} %length_ref.1, bf16[256,2048]{1,0:T(8,128)(2,1)} %q_ref, bf16[256,256]{1,0:T(8,128)(2,1)} %refs_1_.1, bf16[256,256]{1,0:T(8,128)(2,1)} %refs_2_.1), custom_call_target="tpu_custom_call" | custom-call | flops 5750000128 | tf_op jit(solution)/shard_map/pallas_call | solution.py:342
  24.0 0.0 collective-permute-done.2.refs_5_
  24.1 0.0 collective-permute-done.3.refs_6_
  24.1 0.1 collective-permute-start.4
  24.1 2.0 %collective-permute-start.5 = (bf16[256,256]{1,0:T(8,128)(2,1)S(1)}, bf16[256,256]{1,0:T(8,128)(2,1)S(1)}, u32[]{:S(2)}, u32[]{:S(2)}) collective-permute-start(bf16[256,256]{1,0:T(8,128)(2,1)S(1)} %collective-permute-done.3.refs_6_), channel_id=1, source_target_pairs={{0,2},{4,0},{8,4},{12,8},{14,12},{10,14},{6,10},{2,6},{1,3},{5,1},... | collective-permute-start | bytes 393224 | tf_op jit(solution)/shard_map/ppermute | solution.py:637
  26.2 0.0 collective-permute-done.8.refs_12_
  26.2 0.0 collective-permute-done.7.refs_10_
  26.2 0.0 copy-done.3
  26.2 0.1 collective-permute-start.10
  26.2 2.0 %collective-permute-start.9 = (bf16[64,2048]{1,0:T(8,128)(2,1)S(1)}, bf16[64,2048]{1,0:T(8,128)(2,1)S(1)}, u32[]{:S(2)}, u32[]{:S(2)}) collective-permute-start(bf16[64,2048]{1,0:T(8,128)(2,1)S(1)} %copy-done.3), channel_id=1, source_target_pairs={{0,4},{4,8},{8,12},{12,14},{14,10},{10,6},{6,2},{2,0},{1,5},{5,9},... | collective-permute-start | bytes 786440 | tf_op jit(solution)/shard_map/ppermute | solution.py:637
  28.3 0.2 add_reduce_fusion
  28.4 1.9 %collective-permute-done.4.refs_7_ = bf16[256,256]{1,0:T(8,128)(2,1)S(1)} collective-permute-done((bf16[256,256]{1,0:T(8,128)(2,1)S(1)}, bf16[256,256]{1,0:T(8,128)(2,1)S(1)}, u32[]{:S(2)}, u32[]{:S(2)}) %collective-permute-start.4) | collective-permute-done | bytes 131104 | tf_op jit(solution)/shard_map/ppermute | solution.py:637
  30.3 0.3 collective-permute-done.5.refs_8_
  30.6 0.0 collective-permute-start.6
  30.6 0.0 collective-permute-start.11
  30.6 2.0 %collective-permute-start.12 = (bf16[64,2048]{1,0:T(8,128)(2,1)S(1)}, bf16[64,2048]{1,0:T(8,128)(2,1)S(1)}, u32[]{:S(2)}, u32[]{:S(2)}) collective-permute-start(bf16[64,2048]{1,0:T(8,128)(2,1)S(1)} %collective-permute-done.8.refs_12_), channel_id=1, source_target_pairs={{0,2},{4,0},{8,4},{12,8},{14,12},{10,14},{6,10},{2,6},{1,3},{5,1},... | collective-permute-start | bytes 786440 | tf_op jit(solution)/shard_map/ppermute | solution.py:637
  32.7 3.1 %collective-permute-done.10.refs_13_ = bf16[64,2048]{1,0:T(8,128)(2,1)S(1)} collective-permute-done((bf16[64,2048]{1,0:T(8,128)(2,1)S(1)}, bf16[64,2048]{1,0:T(8,128)(2,1)S(1)}, u32[]{:S(2)}, u32[]{:S(2)}) %collective-permute-start.10) | collective-permute-done | bytes 262176 | tf_op jit(solution)/shard_map/ppermute | solution.py:637
  35.7 0.9 collective-permute-done.9.refs_11_
  36.6 0.9 collective-permute-start.13
  37.5 1.1 collective-permute-start.14
  38.6 0.8 collective-permute-done.6.refs_9_
  39.4 0.0 copy-done
  39.4 0.0 copy-done.1
  39.4 23.8 %shard_map.88 = (bf16[1024,256]{1,0:T(8,128)(2,1)}, bf16[1024,256]{1,0:T(8,128)(2,1)}, bf16[1024,256]{1,0:T(8,128)(2,1)S(1)}, bf16[1024,512]{1,0:T(8,128)(2,1)S(1)}, bf16[2,128,2048]{2,1,0:T(8,128)(2,1)S(1)}) custom-call(s32[8]{0:T(128)S(1)} %broadcast_add_fusion.1.refs_0_, bf16[256,256]{1,0:T(8,128)(2,1)S(1)} %copy-done, bf16[256,256]{1,0:T(8,128)(2,1)S(1)} %copy-done.1, ...), custom_call_target="tpu_custom_call" | custom-call | flops 8049999872 | tf_op jit(solution)/shard_map/pallas_call | solution.py:432
  63.2 0.0 collective-permute-done.11.refs_1_
  63.3 0.0 collective-permute-done.12.refs_3_
  63.3 0.1 collective-permute-start.15
  63.3 2.0 %collective-permute-start.16 = (bf16[64,2048]{1,0:T(8,128)(2,1)S(1)}, bf16[64,2048]{1,0:T(8,128)(2,1)S(1)}, u32[]{:S(2)}, u32[]{:S(2)}) collective-permute-start(bf16[64,2048]{1,0:T(8,128)(2,1)S(1)} %collective-permute-done.12.refs_3_), channel_id=1, source_target_pairs={{0,2},{4,0},{8,4},{12,8},{14,12},{10,14},{6,10},{2,6},{1,3},{5,1},... | collective-permute-start | bytes 786440 | tf_op jit(solution)/shard_map/ppermute | solution.py:637
  65.3 0.0 collective-permute-done.13.refs_2_
  65.3 0.0 collective-permute-done.14.refs_4_
  65.4 0.1 collective-permute-start.17
  65.4 2.0 %collective-permute-start.18 = (bf16[64,2048]{1,0:T(8,128)(2,1)S(1)}, bf16[64,2048]{1,0:T(8,128)(2,1)S(1)}, u32[]{:S(2)}, u32[]{:S(2)}) collective-permute-start(bf16[64,2048]{1,0:T(8,128)(2,1)S(1)} %collective-permute-done.14.refs_4_), channel_id=1, source_target_pairs={{0,2},{4,0},{8,4},{12,8},{14,12},{10,14},{6,10},{2,6},{1,3},{5,1},... | collective-permute-start | bytes 786440 | tf_op jit(solution)/shard_map/ppermute | solution.py:637
  67.4 30.3 %shard_map.89.refs_2_ = bf16[2,128,2048]{2,1,0:T(8,128)(2,1)S(1)} custom-call(s32[8]{0:T(128)S(1)} %broadcast_add_fusion.1.refs_0_, bf16[64,2048]{1,0:T(8,128)(2,1)S(1)} %collective-permute-done.11.refs_1_, bf16[64,2048]{1,0:T(8,128)(2,1)S(1)} %collective-permute-done.13.refs_2_, bf16[64,2048]{1,0:T(8,128)(2,1)S(1)} %collective-permute-done.12.refs_3_, ...), custom_call_target="tpu_custom_call" | custom-call | flops 6899999744 | tf_op jit(solution)/shard_map/pallas_call | solution.py:467
  97.7 0.0 collective-permute-done.15.refs_1_
  97.7 0.0 collective-permute-done.16.refs_3_
  97.7 0.1 collective-permute-start.19
  97.7 0.0 collective-permute-done.17.refs_2_
  97.8 0.0 collective-permute-done.18.refs_4_
  97.8 2.0 %collective-permute-start.20 = (bf16[64,2048]{1,0:T(8,128)(2,1)S(1)}, bf16[64,2048]{1,0:T(8,128)(2,1)S(1)}, u32[]{:S(2)}, u32[]{:S(2)}) collective-permute-start(bf16[64,2048]{1,0:T(8,128)(2,1)S(1)} %collective-permute-done.18.refs_4_), channel_id=1, source_target_pairs={{0,2},{4,0},{8,4},{12,8},{14,12},{10,14},{6,10},{2,6},{1,3},{5,1},... | collective-permute-start | bytes 786440 | tf_op jit(solution)/shard_map/ppermute | solution.py:637
  99.8 9.8 %shard_map.90.refs_3_ = bf16[2,128,2048]{2,1,0:T(8,128)(2,1)S(1)} custom-call(s32[8]{0:T(128)S(1)} %broadcast_add_fusion.1.refs_0_, bf16[64,2048]{1,0:T(8,128)(2,1)S(1)} %collective-permute-done.15.refs_1_, bf16[64,2048]{1,0:T(8,128)(2,1)S(1)} %collective-permute-done.17.refs_2_, bf16[64,2048]{1,0:T(8,128)(2,1)S(1)} %collective-permute-done.16.refs_3_, ...), custom_call_target="tpu_custom_call" | custom-call | flops 6899999744 | tf_op jit(solution)/shard_map/pallas_call | solution.py:467
  109.5 0.0 collective-permute-done.19.refs_4_
  109.6 0.0 collective-permute-done.20.refs_5_
  109.6 13.6 %shard_map.91 = bf16[1024,2048]{1,0:T(8,128)(2,1)} custom-call(s32[8]{0:T(128)S(1)} %broadcast_add_fusion.1.refs_0_, bf16[2,128,2048]{2,1,0:T(8,128)(2,1)S(1)} %get-tuple-element.58.refs_1_, bf16[2,128,2048]{2,1,0:T(8,128)(2,1)S(1)} %shard_map.89.refs_2_, bf16[2,128,2048]{2,1,0:T(8,128)(2,1)S(1)} %shard_map.90.refs_3_, ...), custom_call_target="tpu_custom_call", output_to_operand_aliasing={{}: (8, {})} | custom-call | flops 4600000000 | tf_op jit(solution)/shard_map/pallas_call | solution.py:518
  (5 shorter events, 0.0 us)
Async XLA Ops:
  2.2 6.1 %copy-start.4 = (s32[8,2]{0,1:T(2,128)S(1)}, s32[8,2]{0,1:T(2,128)}, u32[]{:S(2)}) copy-start(s32[8,2]{0,1:T(2,128)} %param.10) | copy-start | bytes 196
  2.2 6.1 %copy-start.5 = (s32[8,2]{0,1:T(2,128)S(1)}, s32[8,2]{0,1:T(2,128)}, u32[]{:S(2)}) copy-start(s32[8,2]{0,1:T(2,128)} %param.11) | copy-start | bytes 196
  2.2 6.1 %copy-start.2 = (s32[8]{0:T(128)S(1)}, s32[8]{0:T(128)}, u32[]{:S(2)}) copy-start(s32[8]{0:T(128)} %length_ref.1) | copy-start | bytes 100
  2.2 6.1 %collective-permute-start.1 = (bf16[256,256]{1,0:T(8,128)(2,1)}, bf16[256,256]{1,0:T(8,128)(2,1)S(1)}, u32[]{:S(2)}, u32[]{:S(2)}) collective-permute-start(bf16[256,256]{1,0:T(8,128)(2,1)} %shard_map.85), channel_id=1, source_target_pairs={{0,2},{4,0},{8,4},{12,8},{14,12},{10,14},{6,10},{2,6},{1,3},{5,1},... | collective-permute-start | bytes 393224 | tf_op jit(solution)/shard_map/ppermute | solution.py:637
  3.9 5.2 %collective-permute-start = (bf16[256,256]{1,0:T(8,128)(2,1)}, bf16[256,256]{1,0:T(8,128)(2,1)S(1)}, u32[]{:S(2)}, u32[]{:S(2)}) collective-permute-start(bf16[256,256]{1,0:T(8,128)(2,1)} %shard_map.85), channel_id=1, source_target_pairs={{0,4},{4,8},{8,12},{12,14},{14,10},{10,6},{6,2},{2,0},{1,5},{5,9},... | collective-permute-start | bytes 393224 | tf_op jit(solution)/shard_map/ppermute | solution.py:637
  6.2 20.0 %collective-permute-start.8 = (bf16[64,2048]{1,0:T(8,128)(2,1)}, bf16[64,2048]{1,0:T(8,128)(2,1)S(1)}, u32[]{:S(2)}, u32[]{:S(2)}) collective-permute-start(bf16[64,2048]{1,0:T(8,128)(2,1)} %get-tuple-element.51), channel_id=1, source_target_pairs={{0,2},{4,0},{8,4},{12,8},{14,12},{10,14},{6,10},{2,6},{1,3},{5,1},... | collective-permute-start | bytes 786440 | tf_op jit(solution)/shard_map/ppermute | solution.py:637
  7.8 18.4 %collective-permute-start.7 = (bf16[64,2048]{1,0:T(8,128)(2,1)}, bf16[64,2048]{1,0:T(8,128)(2,1)S(1)}, u32[]{:S(2)}, u32[]{:S(2)}) collective-permute-start(bf16[64,2048]{1,0:T(8,128)(2,1)} %get-tuple-element.51), channel_id=1, source_target_pairs={{0,4},{4,8},{8,12},{12,14},{14,10},{10,6},{6,2},{2,0},{1,5},{5,9},... | collective-permute-start | bytes 786440 | tf_op jit(solution)/shard_map/ppermute | solution.py:637
  8.3 17.8 %copy-start.3 = (bf16[64,2048]{1,0:T(8,128)(2,1)S(1)}, bf16[64,2048]{1,0:T(8,128)(2,1)}, u32[]{:S(2)}) copy-start(bf16[64,2048]{1,0:T(8,128)(2,1)} %get-tuple-element.55) | copy-start | bytes 786436
  8.3 31.1 %copy-start = (bf16[256,256]{1,0:T(8,128)(2,1)S(1)}, bf16[256,256]{1,0:T(8,128)(2,1)}, u32[]{:S(2)}) copy-start(bf16[256,256]{1,0:T(8,128)(2,1)} %refs_1_.1) | copy-start | bytes 393220
  8.3 31.1 %copy-start.1 = (bf16[256,256]{1,0:T(8,128)(2,1)S(1)}, bf16[256,256]{1,0:T(8,128)(2,1)}, u32[]{:S(2)}) copy-start(bf16[256,256]{1,0:T(8,128)(2,1)} %refs_2_.1) | copy-start | bytes 393220
  9.0 15.0 %collective-permute-start.2 = (bf16[256,256]{1,0:T(8,128)(2,1)S(1)}, bf16[256,256]{1,0:T(8,128)(2,1)S(1)}, u32[]{:S(2)}, u32[]{:S(2)}) collective-permute-start(bf16[256,256]{1,0:T(8,128)(2,1)S(1)} %collective-permute-done.refs_3_), channel_id=1, source_target_pairs={{0,4},{4,8},{8,12},{12,14},{14,10},{10,6},{6,2},{2,0},{1,5},{5,9},... | collective-permute-start | bytes 393224 | tf_op jit(solution)/shard_map/ppermute | solution.py:637
  9.5 14.6 %collective-permute-start.3 = (bf16[256,256]{1,0:T(8,128)(2,1)S(1)}, bf16[256,256]{1,0:T(8,128)(2,1)S(1)}, u32[]{:S(2)}, u32[]{:S(2)}) collective-permute-start(bf16[256,256]{1,0:T(8,128)(2,1)S(1)} %collective-permute-done.1.refs_4_), channel_id=1, source_target_pairs={{0,2},{4,0},{8,4},{12,8},{14,12},{10,14},{6,10},{2,6},{1,3},{5,1},... | collective-permute-start | bytes 393224 | tf_op jit(solution)/shard_map/ppermute | solution.py:637
  24.1 6.3 %collective-permute-start.4 = (bf16[256,256]{1,0:T(8,128)(2,1)S(1)}, bf16[256,256]{1,0:T(8,128)(2,1)S(1)}, u32[]{:S(2)}, u32[]{:S(2)}) collective-permute-start(bf16[256,256]{1,0:T(8,128)(2,1)S(1)} %collective-permute-done.2.refs_5_), channel_id=1, source_target_pairs={{0,4},{4,8},{8,12},{12,14},{14,10},{10,6},{6,2},{2,0},{1,5},{5,9},... | collective-permute-start | bytes 393224 | tf_op jit(solution)/shard_map/ppermute | solution.py:637
  24.1 6.5 %collective-permute-start.5 = (bf16[256,256]{1,0:T(8,128)(2,1)S(1)}, bf16[256,256]{1,0:T(8,128)(2,1)S(1)}, u32[]{:S(2)}, u32[]{:S(2)}) collective-permute-start(bf16[256,256]{1,0:T(8,128)(2,1)S(1)} %collective-permute-done.3.refs_6_), channel_id=1, source_target_pairs={{0,2},{4,0},{8,4},{12,8},{14,12},{10,14},{6,10},{2,6},{1,3},{5,1},... | collective-permute-start | bytes 393224 | tf_op jit(solution)/shard_map/ppermute | solution.py:637
  26.2 9.6 %collective-permute-start.10 = (bf16[64,2048]{1,0:T(8,128)(2,1)S(1)}, bf16[64,2048]{1,0:T(8,128)(2,1)S(1)}, u32[]{:S(2)}, u32[]{:S(2)}) collective-permute-start(bf16[64,2048]{1,0:T(8,128)(2,1)S(1)} %copy-done.3), channel_id=1, source_target_pairs={{0,2},{4,0},{8,4},{12,8},{14,12},{10,14},{6,10},{2,6},{1,3},{5,1},... | collective-permute-start | bytes 786440 | tf_op jit(solution)/shard_map/ppermute | solution.py:637
  26.2 10.4 %collective-permute-start.9 = (bf16[64,2048]{1,0:T(8,128)(2,1)S(1)}, bf16[64,2048]{1,0:T(8,128)(2,1)S(1)}, u32[]{:S(2)}, u32[]{:S(2)}) collective-permute-start(bf16[64,2048]{1,0:T(8,128)(2,1)S(1)} %copy-done.3), channel_id=1, source_target_pairs={{0,4},{4,8},{8,12},{12,14},{14,10},{10,6},{6,2},{2,0},{1,5},{5,9},... | collective-permute-start | bytes 786440 | tf_op jit(solution)/shard_map/ppermute | solution.py:637
  30.6 8.8 %collective-permute-start.6 = (bf16[256,256]{1,0:T(8,128)(2,1)S(1)}, bf16[256,256]{1,0:T(8,128)(2,1)S(1)}, u32[]{:S(2)}, u32[]{:S(2)}) collective-permute-start(bf16[256,256]{1,0:T(8,128)(2,1)S(1)} %collective-permute-done.4.refs_7_), channel_id=1, source_target_pairs={{0,4},{4,8},{8,12},{12,14},{14,10},{10,6},{6,2},{2,0},{1,5},{5,9},... | collective-permute-start | bytes 393224 | tf_op jit(solution)/shard_map/ppermute | solution.py:637
  30.6 32.6 %collective-permute-start.11 = (bf16[64,2048]{1,0:T(8,128)(2,1)S(1)}, bf16[64,2048]{1,0:T(8,128)(2,1)S(1)}, u32[]{:S(2)}, u32[]{:S(2)}) collective-permute-start(bf16[64,2048]{1,0:T(8,128)(2,1)S(1)} %collective-permute-done.7.refs_10_), channel_id=1, source_target_pairs={{0,4},{4,8},{8,12},{12,14},{14,10},{10,6},{6,2},{2,0},{1,5},{5,9},... | collective-permute-start | bytes 786440 | tf_op jit(solution)/shard_map/ppermute | solution.py:637
  30.6 32.6 %collective-permute-start.12 = (bf16[64,2048]{1,0:T(8,128)(2,1)S(1)}, bf16[64,2048]{1,0:T(8,128)(2,1)S(1)}, u32[]{:S(2)}, u32[]{:S(2)}) collective-permute-start(bf16[64,2048]{1,0:T(8,128)(2,1)S(1)} %collective-permute-done.8.refs_12_), channel_id=1, source_target_pairs={{0,2},{4,0},{8,4},{12,8},{14,12},{10,14},{6,10},{2,6},{1,3},{5,1},... | collective-permute-start | bytes 786440 | tf_op jit(solution)/shard_map/ppermute | solution.py:637
  36.6 28.8 %collective-permute-start.13 = (bf16[64,2048]{1,0:T(8,128)(2,1)S(1)}, bf16[64,2048]{1,0:T(8,128)(2,1)S(1)}, u32[]{:S(2)}, u32[]{:S(2)}) collective-permute-start(bf16[64,2048]{1,0:T(8,128)(2,1)S(1)} %collective-permute-done.9.refs_11_), channel_id=1, source_target_pairs={{0,4},{4,8},{8,12},{12,14},{14,10},{10,6},{6,2},{2,0},{1,5},{5,9},... | collective-permute-start | bytes 786440 | tf_op jit(solution)/shard_map/ppermute | solution.py:637
  37.5 27.9 %collective-permute-start.14 = (bf16[64,2048]{1,0:T(8,128)(2,1)S(1)}, bf16[64,2048]{1,0:T(8,128)(2,1)S(1)}, u32[]{:S(2)}, u32[]{:S(2)}) collective-permute-start(bf16[64,2048]{1,0:T(8,128)(2,1)S(1)} %collective-permute-done.10.refs_13_), channel_id=1, source_target_pairs={{0,2},{4,0},{8,4},{12,8},{14,12},{10,14},{6,10},{2,6},{1,3},{5,1},... | collective-permute-start | bytes 786440 | tf_op jit(solution)/shard_map/ppermute | solution.py:637
  63.3 34.4 %collective-permute-start.15 = (bf16[64,2048]{1,0:T(8,128)(2,1)S(1)}, bf16[64,2048]{1,0:T(8,128)(2,1)S(1)}, u32[]{:S(2)}, u32[]{:S(2)}) collective-permute-start(bf16[64,2048]{1,0:T(8,128)(2,1)S(1)} %collective-permute-done.11.refs_1_), channel_id=1, source_target_pairs={{0,4},{4,8},{8,12},{12,14},{14,10},{10,6},{6,2},{2,0},{1,5},{5,9},... | collective-permute-start | bytes 786440 | tf_op jit(solution)/shard_map/ppermute | solution.py:637
  63.3 34.3 %collective-permute-start.16 = (bf16[64,2048]{1,0:T(8,128)(2,1)S(1)}, bf16[64,2048]{1,0:T(8,128)(2,1)S(1)}, u32[]{:S(2)}, u32[]{:S(2)}) collective-permute-start(bf16[64,2048]{1,0:T(8,128)(2,1)S(1)} %collective-permute-done.12.refs_3_), channel_id=1, source_target_pairs={{0,2},{4,0},{8,4},{12,8},{14,12},{10,14},{6,10},{2,6},{1,3},{5,1},... | collective-permute-start | bytes 786440 | tf_op jit(solution)/shard_map/ppermute | solution.py:637
  65.4 32.4 %collective-permute-start.17 = (bf16[64,2048]{1,0:T(8,128)(2,1)S(1)}, bf16[64,2048]{1,0:T(8,128)(2,1)S(1)}, u32[]{:S(2)}, u32[]{:S(2)}) collective-permute-start(bf16[64,2048]{1,0:T(8,128)(2,1)S(1)} %collective-permute-done.13.refs_2_), channel_id=1, source_target_pairs={{0,4},{4,8},{8,12},{12,14},{14,10},{10,6},{6,2},{2,0},{1,5},{5,9},... | collective-permute-start | bytes 786440 | tf_op jit(solution)/shard_map/ppermute | solution.py:637
  65.4 32.3 %collective-permute-start.18 = (bf16[64,2048]{1,0:T(8,128)(2,1)S(1)}, bf16[64,2048]{1,0:T(8,128)(2,1)S(1)}, u32[]{:S(2)}, u32[]{:S(2)}) collective-permute-start(bf16[64,2048]{1,0:T(8,128)(2,1)S(1)} %collective-permute-done.14.refs_4_), channel_id=1, source_target_pairs={{0,2},{4,0},{8,4},{12,8},{14,12},{10,14},{6,10},{2,6},{1,3},{5,1},... | collective-permute-start | bytes 786440 | tf_op jit(solution)/shard_map/ppermute | solution.py:637
  97.7 11.9 %collective-permute-start.19 = (bf16[64,2048]{1,0:T(8,128)(2,1)S(1)}, bf16[64,2048]{1,0:T(8,128)(2,1)S(1)}, u32[]{:S(2)}, u32[]{:S(2)}) collective-permute-start(bf16[64,2048]{1,0:T(8,128)(2,1)S(1)} %collective-permute-done.15.refs_1_), channel_id=1, source_target_pairs={{0,4},{4,8},{8,12},{12,14},{14,10},{10,6},{6,2},{2,0},{1,5},{5,9},... | collective-permute-start | bytes 786440 | tf_op jit(solution)/shard_map/ppermute | solution.py:637
  97.8 11.8 %collective-permute-start.20 = (bf16[64,2048]{1,0:T(8,128)(2,1)S(1)}, bf16[64,2048]{1,0:T(8,128)(2,1)S(1)}, u32[]{:S(2)}, u32[]{:S(2)}) collective-permute-start(bf16[64,2048]{1,0:T(8,128)(2,1)S(1)} %collective-permute-done.18.refs_4_), channel_id=1, source_target_pairs={{0,2},{4,0},{8,4},{12,8},{14,12},{10,14},{6,10},{2,6},{1,3},{5,1},... | collective-permute-start | bytes 786440 | tf_op jit(solution)/shard_map/ppermute | solution.py:637
where the time goes:
time: 124 us; the launch traced here: 123 us
  Pallas kernels  93.9 us (76%)
  starting transfers between devices  20.6 us (17%)
  waiting for transfers between devices  7.58 us (6%)
    pallas_call x2, Pallas kernels, attend_later(): pl.pallas_call(lambda *refs: later_kernel(offsets, pieces, *refs), out_sh...  40 us
    pallas_call x1, Pallas kernels, attend_first(): pl.pallas_call(lambda *refs: first_kernel(kv_offsets, offsets, pieces, *r...  23.8 us
    ppermute x21, starting transfers between devices, shift(): return lax.ppermute(block, 'replica', pairs)  20.6 us
    pallas_call x1, Pallas kernels, attend_last(): pl.pallas_call(lambda *refs: last_kernel(before, offsets, pieces, *refs),...  13.6 us
    pallas_call x1, Pallas kernels, attend_local(): pl.pallas_call(local_kernel, out_shape=jax.ShapeDtypeStruct((MAXC * SPAN,...  13 us
    ppermute x21, waiting for transfers between devices, shift(): return lax.ppermute(block, 'replica', pairs)  7.58 us
  transfers between devices with their start and end apart: 21, of which 6 were waited for; matrix products, arithmetic and copies ran while one was open for 0% of the time, Pallas kernels for 64%

commit v1 on v0

--- a/solution.py
+++ b/solution.py
@@ -17,6 +17,7 @@
 LOG2E = 1.0 / math.log(2.0)
 VMEM_BYTES = 40 * 1024 * 1024
 MOST_VMEM_BYTES = 60 * 1024 * 1024
+LOCAL_VMEM_BYTES = 56 * 1024 * 1024
 LEAST_SUM, MOST_SUM = 1e-20, 1e30
 ANY = pl.BlockSpec(memory_space=pl.ANY)
 SMEM = pl.BlockSpec(memory_space=pltpu.SMEM)
@@ -31,68 +32,54 @@
     return list(range(0, replicas, 2)) + list(range(replicas - 1, 0, -2))
 
 
-def pass_on(fetches, stores):
-    for copy in fetches:
+def copy_all(copies):
+    for copy in copies:
         copy.start()
-    for copy in fetches:
+    for copy in copies:
         copy.wait()
-    for copy in stores:
-        copy.start()
-    for copy in stores:
-        copy.wait()
-
-
-def pack_kv_kernel(k_ref, v_ref, o_ref, buf, sems):
-    pass_on(
+
+
+def pack_kv_kernel(k_ref, v_ref, o_ref, sems):
+    copy_all(
         [
-            pltpu.make_async_copy(k_ref.at[SPAN:], buf.at[:SPAN], sems.at[0]),
-            pltpu.make_async_copy(v_ref.at[SPAN:], buf.at[SPAN:], sems.at[1]),
-        ],
-        [pltpu.make_async_copy(buf, o_ref, sems.at[2])],
+            pltpu.make_async_copy(k_ref.at[SPAN:], o_ref.at[:SPAN], sems.at[0]),
+            pltpu.make_async_copy(v_ref.at[SPAN:], o_ref.at[SPAN:], sems.at[1]),
+        ]
     )
 
 
 def pack_kv(keys, values):
-    shape = (2 * SPAN, keys.shape[1])
     return pl.pallas_call(
         pack_kv_kernel,
-        out_shape=jax.ShapeDtypeStruct(shape, keys.dtype),
+        out_shape=jax.ShapeDtypeStruct((2 * SPAN, keys.shape[1]), keys.dtype),
         in_specs=[ANY] * 2,
-        out_specs=ANY,
-        scratch_shapes=[pltpu.VMEM(shape, keys.dtype), pltpu.SemaphoreType.DMA((3,))],
+        out_specs=VMEM,
+        scratch_shapes=[pltpu.SemaphoreType.DMA((2,))],
         compiler_params=pltpu.CompilerParams(vmem_limit_bytes=MOST_VMEM_BYTES),
-        cost_estimate=cost_of(1.7),
+        cost_estimate=cost_of(1),
     )(keys, values)
 
 
-def pack_q_kernel(q_ref, o_top, o_bottom, buf, sems):
+def pack_q_kernel(q_ref, o_top, o_bottom, sems):
     half = SPAN // 2
-    pass_on(
+    copy_all(
         [
-            pltpu.make_async_copy(q_ref.at[SPAN : SPAN + half], buf.at[:half], sems.at[0]),
-            pltpu.make_async_copy(q_ref.at[SPAN + half :], buf.at[half:], sems.at[1]),
-        ],
-        [
-            pltpu.make_async_copy(buf.at[:half], o_top, sems.at[2]),
-            pltpu.make_async_copy(buf.at[half:], o_bottom, sems.at[3]),
-        ],
+            pltpu.make_async_copy(q_ref.at[SPAN : SPAN + half], o_top, sems.at[0]),
+            pltpu.make_async_copy(q_ref.at[SPAN + half :], o_bottom, sems.at[1]),
+        ]
     )
 
 
 def pack_q(queries):
-    width = queries.shape[1]
-    half = jax.ShapeDtypeStruct((SPAN // 2, width), queries.dtype)
+    half = jax.ShapeDtypeStruct((SPAN // 2, queries.shape[1]), queries.dtype)
     return pl.pallas_call(
         pack_q_kernel,
         out_shape=(half, half),
         in_specs=[ANY],
-        out_specs=(ANY, ANY),
-        scratch_shapes=[
-            pltpu.VMEM((SPAN, width), queries.dtype),
-            pltpu.SemaphoreType.DMA((4,)),
-        ],
+        out_specs=(VMEM, VMEM),
+        scratch_shapes=[pltpu.SemaphoreType.DMA((2,))],
         compiler_params=pltpu.CompilerParams(vmem_limit_bytes=MOST_VMEM_BYTES),
-        cost_estimate=cost_of(1.7),
+        cost_estimate=cost_of(1),
     )(queries)
 
 
@@ -305,57 +292,52 @@
     return lambda j, span: pltpu.make_async_copy(buf.at[j], o_ref.at[rows_of(span)], sems.at[j])
 
 
-def local_kernel(length_ref, q_hbm, k_hbm, v_hbm, o_ref, q_ref, k_ref, v_ref, wide, zeros, sems, out_buf, out_sems, *work):
+def local_kernel(length_ref, q_hbm, k_hbm, v_hbm, out_buf, q_ref, k_ref, v_ref, wide, sems, *work):
     live = length_ref[lax.axis_index("replica")]
+
+    def fetch(slot):
+        rows = slice(slot * SPAN, (slot + 1) * SPAN)
+        return pltpu.make_async_copy(q_hbm.at[rows], q_ref.at[rows], sems.at[2 + slot])
+
     fetches = [
         pltpu.make_async_copy(k_hbm, k_ref, sems.at[0]),
-        pltpu.make_async_copy(v_hbm, v_ref, sems.at[MAXC]),
-        pltpu.make_async_copy(q_hbm, q_ref, sems.at[MAXC + 1]),
+        pltpu.make_async_copy(v_hbm, v_ref, sems.at[1]),
+        fetch(0),
     ]
     for copy in fetches:
         copy.start()
-    zeros[...] = jnp.zeros_like(zeros)
-
-    def clear(span):
-        return pltpu.make_async_copy(zeros, o_ref.at[rows_of(span)], sems.at[span])
-
-    for span in range(1, MAXC):
-        pl.when(span >= live)(clear(span).start)
+    pl.when(live > 1)(fetch(1).start)
     for copy in fetches:
         copy.wait()
     widen(v_ref, wide)
+    pl.when(live > 1)(fetch(1).wait)
     attend_blocks(
         [jnp.int32(0), jnp.where(live > 1, 1, -1)],
         [(q_ref.at[:SPAN],), (q_ref.at[SPAN:],)],
         k_ref,
         wide,
         out_buf,
-        stores(out_buf, o_ref, out_sems),
+        None,
         *work,
     )
-    for span in range(1, MAXC):
-        pl.when(span >= live)(clear(span).wait)
 
 
 def attend_local(lengths, queries, keys, values):
     width, key_width = queries.shape[1], keys.shape[1]
     return pl.pallas_call(
         local_kernel,
-        out_shape=jax.ShapeDtypeStruct((MAXC * SPAN, width), queries.dtype),
+        out_shape=jax.ShapeDtypeStruct((SLOTS, SPAN, width), queries.dtype),
         in_specs=[SMEM, ANY, ANY, ANY],
-        out_specs=ANY,
+        out_specs=VMEM,
         scratch_shapes=[
             pltpu.VMEM(queries.shape, queries.dtype),
             pltpu.VMEM(keys.shape, keys.dtype),
             pltpu.VMEM(values.shape, values.dtype),
             pltpu.VMEM((SLOTS * SPAN, 2 * key_width), keys.dtype),
-            pltpu.VMEM((SPAN, width), queries.dtype),
-            pltpu.SemaphoreType.DMA((MAXC + 2,)),
-            pltpu.VMEM((SLOTS, SPAN, width), queries.dtype),
-            pltpu.SemaphoreType.DMA((SLOTS,)),
+            pltpu.SemaphoreType.DMA((2 + SLOTS,)),
             *work_space(SLOTS, width, key_width),
         ],
-        compiler_params=pltpu.CompilerParams(vmem_limit_bytes=MOST_VMEM_BYTES),
+        compiler_params=pltpu.CompilerParams(vmem_limit_bytes=LOCAL_VMEM_BYTES),
         cost_estimate=cost_of(5),
     )(lengths, queries, keys, values)
 
@@ -372,7 +354,7 @@
     parts = sum(pieces)
     blocks, refs = refs[: len(kv_offsets)], refs[len(kv_offsets) :]
     q_refs, refs = refs[:parts], refs[parts:]
-    o_k, o_v, k_buf, wide, out_buf, v_buf, in_sems, out_sems, *work = refs
+    local, o_k, o_v, k_buf, wide, out_buf, o_ref, v_buf, zeros, in_sems, out_sems, span_sems, *work = refs
     live = meta_ref[0]
 
     def fetches():
@@ -389,7 +371,18 @@
             else:
                 pl.when(needed)(copy)
 
+    def each_span(act):
+        for span in range(MAXC):
+            there, sem = o_ref.at[rows_of(span)], span_sems.at[span]
+            if span < SLOTS:
+                copy = pltpu.make_async_copy(local.at[span], there, sem)
+                pl.when(span < live)(getattr(copy, act))
+            if span > 0:
+                pl.when(span >= live)(getattr(pltpu.make_async_copy(zeros, there, sem), act))
+
     each("start")
+    zeros[...] = jnp.zeros_like(zeros)
+    each_span("start")
     for span in range(1, MAXC):
 
         @pl.when(span >= live)
@@ -422,9 +415,10 @@
 
     copy_k.wait()
     copy_v.wait()
-
-
-def attend_first(meta, keys, values, kv_offsets, kv_blocks, offsets, blocks):
+    each_span("wait")
+
+
+def attend_first(meta, keys, values, kv_offsets, kv_blocks, offsets, blocks, local):
     rows, key_width = MAXC * SPAN, keys.shape[1]
     pieces = [len(block) for block in blocks]
     count, width = len(pieces), blocks[0][0].shape[1]
@@ -437,18 +431,21 @@
             out,
             jax.ShapeDtypeStruct((rows, 2 * key_width), keys.dtype),
             jax.ShapeDtypeStruct((count, SPAN, width), keys.dtype),
+            jax.ShapeDtypeStruct((rows, width), keys.dtype),
         ),
-        in_specs=[SMEM, ANY, ANY] + [VMEM] * (len(kv_blocks) + sum(pieces)),
-        out_specs=(ANY, ANY, VMEM, VMEM, VMEM),
+        in_specs=[SMEM, ANY, ANY] + [VMEM] * (len(kv_blocks) + sum(pieces) + 1),
+        out_specs=(ANY, ANY, VMEM, VMEM, VMEM, ANY),
         scratch_shapes=[
             pltpu.VMEM((rows, key_width), keys.dtype),
+            pltpu.VMEM((SPAN, width), keys.dtype),
             pltpu.SemaphoreType.DMA((4,)),
             pltpu.SemaphoreType.DMA((2,)),
+            pltpu.SemaphoreType.DMA((MAXC,)),
             *work_space(count, width, key_width),
         ],
         compiler_params=pltpu.CompilerParams(vmem_limit_bytes=VMEM_BYTES),
         cost_estimate=cost_of(1 * (2 + 2.5 * count)),
-    )(meta, keys, values, *kv_blocks, *[part for block in blocks for part in block])
+    )(meta, keys, values, *kv_blocks, *[part for block in blocks for part in block], local)
 
 
 def later_kernel(offsets, pieces, meta_ref, *refs):
@@ -647,9 +644,9 @@
     top.append(joined(go_on(top[0])))
     kv[1] = joined(kv[1])
     kv.append(joined(go_on(kv[1])))
-    attention = attend_local(lengths, after(queries, kv[1]), keys, values)
+    local = attend_local(lengths, after(queries, kv[1]), keys, values)
     bottom.append(joined(go_on([after(block, top[1]) for block in bottom[0]])))
-    kv.append(joined(go_on([after(block, attention) for block in kv[2]])))
+    kv.append(joined(go_on([after(block, local) for block in kv[2]])))
     top.append(joined(go_on([after(block, kv[3]) for block in top[1]])))
     kv.append([shift(kv[3][0], 1)])
     bottom.append(joined(go_on([after(block, kv[3]) for block in bottom[1]])))
@@ -659,8 +656,15 @@
     def blocks(n):
         return list(zip(top[n], bottom[n], strict=True))
 
-    cache_keys, cache_values, ordered_keys, wide_values, result = attend_first(
-        meta, keys, values, sum(offsets, []) + [farthest], sum(kv[1:], []), offsets[0], blocks(1)
+    cache_keys, cache_values, ordered_keys, wide_values, result, attention = attend_first(
+        meta,
+        keys,
+        values,
+        sum(offsets, []) + [farthest],
+        sum(kv[1:], []),
+        offsets[0],
+        blocks(1),
+        local,
     )
     results = [result]
     top.append(joined(go_on(top[2])))

time: 124 us -> 123 us (level)
  the two profiles are of different devices: /device:TPU:2 before, /device:TPU:30 now
where the time goes in v1:
time: 123 us
  Pallas kernels  93.3 us (76%)
  starting transfers between devices  22.1 us (18%)
  waiting for transfers between devices  5.01 us (4%)
  local copies, waits for them, and re-layouts  1.26 us (1%)
    pallas_call x2, Pallas kernels, attend_later(): pl.pallas_call(lambda *refs: later_kernel(offsets, pieces, *refs), out_sh...  40 us
    pallas_call x1, Pallas kernels, attend_first(): pl.pallas_call(lambda *refs: first_kernel(kv_offsets, offsets, pieces, *r...  23.9 us
    ppermute x21, starting transfers between devices, shift(): return lax.ppermute(block, 'replica', pairs)  22.1 us
    pallas_call x1, Pallas kernels, attend_last(): pl.pallas_call(lambda *refs: last_kernel(before, offsets, pieces, *refs),...  13.6 us
    pallas_call x1, Pallas kernels, attend_local(): pl.pallas_call(local_kernel, out_shape=jax.ShapeDtypeStruct((SLOTS, SPAN,...  12.4 us
    ppermute x21, waiting for transfers between devices, shift(): return lax.ppermute(block, 'replica', pairs)  5.01 us
  transfers between devices with their start and end apart: 21, of which 4 were waited for; matrix products, arithmetic and copies ran while one was open for 0% of the time, Pallas kernels for 64%

profile of v1, /device:TPU:30, one launch (start us, length us, event | category | flops | bytes accessed | tf_op | source)
XLA Modules:
  0.0 123.0 jit_solution(2477247698177434713)
XLA Ops:
  0.6 0.0 copy-start.5
  0.6 0.0 copy-start.6
  0.7 0.0 copy-start.3
  0.7 1.6 %shard_map.85 = bf16[256,256]{1,0:T(8,128)(2,1)} custom-call(bf16[256,256]{1,0:T(8,128)(2,1)} %refs_1_.1, bf16[256,256]{1,0:T(8,128)(2,1)} %refs_2_.1), custom_call_target="tpu_custom_call" | custom-call | flops 1150000000 | tf_op jit(solution)/shard_map/pallas_call | solution.py:52
  2.2 0.6 collective-permute-start.1
  2.8 1.5 %collective-permute-start = (bf16[256,256]{1,0:T(8,128)(2,1)}, bf16[256,256]{1,0:T(8,128)(2,1)S(1)}, u32[]{:S(2)}, u32[]{:S(2)}) collective-permute-start(bf16[256,256]{1,0:T(8,128)(2,1)} %shard_map.85), channel_id=1, source_target_pairs={{0,4},{4,8},{8,12},{12,14},{14,10},{10,6},{6,2},{2,0},{1,5},{5,9},... | collective-permute-start | bytes 393224 | tf_op jit(solution)/shard_map/ppermute | solution.py:634
  4.3 1.8 %shard_map.87 = (bf16[64,2048]{1,0:T(8,128)(2,1)}, bf16[64,2048]{1,0:T(8,128)(2,1)}) custom-call(bf16[256,2048]{1,0:T(8,128)(2,1)} %q_ref), custom_call_target="tpu_custom_call" | custom-call | flops 1150000000 | tf_op jit(solution)/shard_map/pallas_call | solution.py:75
  6.1 0.6 collective-permute-start.8
  6.7 1.5 %collective-permute-start.7 = (bf16[64,2048]{1,0:T(8,128)(2,1)}, bf16[64,2048]{1,0:T(8,128)(2,1)S(1)}, u32[]{:S(2)}, u32[]{:S(2)}) collective-permute-start(bf16[64,2048]{1,0:T(8,128)(2,1)} %get-tuple-element.52), channel_id=1, source_target_pairs={{0,4},{4,8},{8,12},{12,14},{14,10},{10,6},{6,2},{2,0},{1,5},{5,9},... | collective-permute-start | bytes 786440 | tf_op jit(solution)/shard_map/ppermute | solution.py:634
  8.2 0.0 copy-done.5
  8.2 0.0 copy-done.6
  8.3 0.0 copy-done.3
  8.3 0.0 copy-start.4
  8.3 0.0 copy-start
  8.3 0.0 copy-start.1
  8.3 0.0 collective-permute-done.1.refs_4_
  8.4 0.0 collective-permute-done.refs_3_
  8.4 1.1 collective-permute-start.2
  9.5 1.0 collective-permute-start.3
  10.4 12.4 %shard_map.86.refs_14_ = bf16[2,128,2048]{2,1,0:T(8,128)(2,1)} custom-call(s32[8]{0:T(128)} %length_ref.1, bf16[256,2048]{1,0:T(8,128)(2,1)} %q_ref, bf16[256,256]{1,0:T(8,128)(2,1)} %refs_1_.1, bf16[256,256]{1,0:T(8,128)(2,1)} %refs_2_.1), custom_call_target="tpu_custom_call" | custom-call | flops 5750000128 | tf_op jit(solution)/shard_map/pallas_call | solution.py:327
  22.8 0.0 collective-permute-done.2.refs_5_
  22.9 0.0 collective-permute-done.3.refs_6_
  22.9 0.1 collective-permute-start.4
  22.9 2.0 %collective-permute-start.5 = (bf16[256,256]{1,0:T(8,128)(2,1)S(1)}, bf16[256,256]{1,0:T(8,128)(2,1)S(1)}, u32[]{:S(2)}, u32[]{:S(2)}) collective-permute-start(bf16[256,256]{1,0:T(8,128)(2,1)S(1)} %collective-permute-done.3.refs_6_), channel_id=1, source_target_pairs={{0,2},{4,0},{8,4},{12,8},{14,12},{10,14},{6,10},{2,6},{1,3},{5,1},... | collective-permute-start | bytes 393224 | tf_op jit(solution)/shard_map/ppermute | solution.py:634
  24.9 0.0 collective-permute-done.8.refs_12_
  25.0 0.0 collective-permute-done.7.refs_10_
  25.0 0.0 copy-done.4
  25.0 0.1 collective-permute-start.10
  25.0 2.0 %collective-permute-start.9 = (bf16[64,2048]{1,0:T(8,128)(2,1)S(1)}, bf16[64,2048]{1,0:T(8,128)(2,1)S(1)}, u32[]{:S(2)}, u32[]{:S(2)}) collective-permute-start(bf16[64,2048]{1,0:T(8,128)(2,1)S(1)} %copy-done.4), channel_id=1, source_target_pairs={{0,4},{4,8},{8,12},{12,14},{14,10},{10,6},{6,2},{2,0},{1,5},{5,9},... | collective-permute-start | bytes 786440 | tf_op jit(solution)/shard_map/ppermute | solution.py:634
  27.0 0.2 add_reduce_fusion
  27.2 2.1 %collective-permute-done.4.refs_7_ = bf16[256,256]{1,0:T(8,128)(2,1)S(1)} collective-permute-done((bf16[256,256]{1,0:T(8,128)(2,1)S(1)}, bf16[256,256]{1,0:T(8,128)(2,1)S(1)}, u32[]{:S(2)}, u32[]{:S(2)}) %collective-permute-start.4) | collective-permute-done | bytes 131104 | tf_op jit(solution)/shard_map/ppermute | solution.py:634
  29.3 0.1 collective-permute-done.5.refs_8_
  29.4 1.5 %collective-permute-start.6 = (bf16[256,256]{1,0:T(8,128)(2,1)S(1)}, bf16[256,256]{1,0:T(8,128)(2,1)S(1)}, u32[]{:S(2)}, u32[]{:S(2)}) collective-permute-start(bf16[256,256]{1,0:T(8,128)(2,1)S(1)} %collective-permute-done.4.refs_7_), channel_id=1, source_target_pairs={{0,4},{4,8},{8,12},{12,14},{14,10},{10,6},{6,2},{2,0},{1,5},{5,9},... | collective-permute-start | bytes 393224 | tf_op jit(solution)/shard_map/ppermute | solution.py:634
  30.9 0.0 collective-permute-start.11
  30.9 2.0 %collective-permute-start.12 = (bf16[64,2048]{1,0:T(8,128)(2,1)S(1)}, bf16[64,2048]{1,0:T(8,128)(2,1)S(1)}, u32[]{:S(2)}, u32[]{:S(2)}) collective-permute-start(bf16[64,2048]{1,0:T(8,128)(2,1)S(1)} %collective-permute-done.8.refs_12_), channel_id=1, source_target_pairs={{0,2},{4,0},{8,4},{12,8},{14,12},{10,14},{6,10},{2,6},{1,3},{5,1},... | collective-permute-start | bytes 786440 | tf_op jit(solution)/shard_map/ppermute | solution.py:634
  32.9 2.1 %collective-permute-done.10.refs_13_ = bf16[64,2048]{1,0:T(8,128)(2,1)S(1)} collective-permute-done((bf16[64,2048]{1,0:T(8,128)(2,1)S(1)}, bf16[64,2048]{1,0:T(8,128)(2,1)S(1)}, u32[]{:S(2)}, u32[]{:S(2)}) %collective-permute-start.10) | collective-permute-done | bytes 262176 | tf_op jit(solution)/shard_map/ppermute | solution.py:634
  35.0 0.0 collective-permute-done.9.refs_11_
  35.0 1.5 %collective-permute-start.13 = (bf16[64,2048]{1,0:T(8,128)(2,1)S(1)}, bf16[64,2048]{1,0:T(8,128)(2,1)S(1)}, u32[]{:S(2)}, u32[]{:S(2)}) collective-permute-start(bf16[64,2048]{1,0:T(8,128)(2,1)S(1)} %collective-permute-done.9.refs_11_), channel_id=1, source_target_pairs={{0,4},{4,8},{8,12},{12,14},{14,10},{10,6},{6,2},{2,0},{1,5},{5,9},... | collective-permute-start | bytes 786440 | tf_op jit(solution)/shard_map/ppermute | solution.py:634
  36.5 0.6 collective-permute-start.14
  37.0 0.7 collective-permute-done.6.refs_9_
  37.7 0.0 copy-done
  37.7 0.0 copy-done.1
  37.7 0.0 copy-start.2
  37.7 1.2 copy-done.2
  39.0 23.9 %shard_map.88 = (bf16[1024,256]{1,0:T(8,128)(2,1)}, bf16[1024,256]{1,0:T(8,128)(2,1)}, bf16[1024,256]{1,0:T(8,128)(2,1)S(1)}, bf16[1024,512]{1,0:T(8,128)(2,1)S(...) custom-call(s32[8]{0:T(128)S(1)} %broadcast_add_fusion.1.refs_0_, bf16[256,256]{1,0:T(8,128)(2,1)S(1)} %copy-done, ...), custom_call_target="tpu_custom_call" | custom-call | flops 8049999872 | tf_op jit(solution)/shard_map/pallas_call | solution.py:426
  62.9 0.0 collective-permute-done.11.refs_1_
  62.9 0.0 collective-permute-done.12.refs_3_
  62.9 0.1 collective-permute-start.15
  63.0 2.0 %collective-permute-start.16 = (bf16[64,2048]{1,0:T(8,128)(2,1)S(1)}, bf16[64,2048]{1,0:T(8,128)(2,1)S(1)}, u32[]{:S(2)}, u32[]{:S(2)}) collective-permute-start(bf16[64,2048]{1,0:T(8,128)(2,1)S(1)} %collective-permute-done.12.refs_3_), channel_id=1, source_target_pairs={{0,2},{4,0},{8,4},{12,8},{14,12},{10,14},{6,10},{2,6},{1,3},{5,1},... | collective-permute-start | bytes 786440 | tf_op jit(solution)/shard_map/ppermute | solution.py:634
  65.0 0.0 collective-permute-done.13.refs_2_
  65.0 0.0 collective-permute-done.14.refs_4_
  65.0 0.1 collective-permute-start.17
  65.1 2.0 %collective-permute-start.18 = (bf16[64,2048]{1,0:T(8,128)(2,1)S(1)}, bf16[64,2048]{1,0:T(8,128)(2,1)S(1)}, u32[]{:S(2)}, u32[]{:S(2)}) collective-permute-start(bf16[64,2048]{1,0:T(8,128)(2,1)S(1)} %collective-permute-done.14.refs_4_), channel_id=1, source_target_pairs={{0,2},{4,0},{8,4},{12,8},{14,12},{10,14},{6,10},{2,6},{1,3},{5,1},... | collective-permute-start | bytes 786440 | tf_op jit(solution)/shard_map/ppermute | solution.py:634
  67.1 17.5 %shard_map.89.refs_2_ = bf16[2,128,2048]{2,1,0:T(8,128)(2,1)S(1)} custom-call(s32[8]{0:T(128)S(1)} %broadcast_add_fusion.1.refs_0_, bf16[64,2048]{1,0:T(8,128)(2,1)S(1)} %collective-permute-done.11.refs_1_, bf16[64,2048]{1,0:T(8,128)(2,1)S(1)} %collective-permute-done.13.refs_2_, bf16[64,2048]{1,0:T(8,128)(2,1)S(1)} %collective-permute-done.12.refs_3_, ...), custom_call_target="tpu_custom_call" | custom-call | flops 6899999744 | tf_op jit(solution)/shard_map/pallas_call | solution.py:464
  84.6 0.0 collective-permute-done.15.refs_1_
  84.6 0.0 collective-permute-done.16.refs_3_
  84.6 0.1 collective-permute-start.19
  84.7 0.0 collective-permute-done.17.refs_2_
  84.7 0.0 collective-permute-done.18.refs_4_
  84.7 2.0 %collective-permute-start.20 = (bf16[64,2048]{1,0:T(8,128)(2,1)S(1)}, bf16[64,2048]{1,0:T(8,128)(2,1)S(1)}, u32[]{:S(2)}, u32[]{:S(2)}) collective-permute-start(bf16[64,2048]{1,0:T(8,128)(2,1)S(1)} %collective-permute-done.18.refs_4_), channel_id=1, source_target_pairs={{0,2},{4,0},{8,4},{12,8},{14,12},{10,14},{6,10},{2,6},{1,3},{5,1},... | collective-permute-start | bytes 786440 | tf_op jit(solution)/shard_map/ppermute | solution.py:634
  86.7 22.5 %shard_map.90.refs_3_ = bf16[2,128,2048]{2,1,0:T(8,128)(2,1)S(1)} custom-call(s32[8]{0:T(128)S(1)} %broadcast_add_fusion.1.refs_0_, bf16[64,2048]{1,0:T(8,128)(2,1)S(1)} %collective-permute-done.15.refs_1_, bf16[64,2048]{1,0:T(8,128)(2,1)S(1)} %collective-permute-done.17.refs_2_, bf16[64,2048]{1,0:T(8,128)(2,1)S(1)} %collective-permute-done.16.refs_3_, ...), custom_call_target="tpu_custom_call" | custom-call | flops 6899999744 | tf_op jit(solution)/shard_map/pallas_call | solution.py:464
  109.2 0.0 collective-permute-done.19.refs_4_
  109.2 0.0 collective-permute-done.20.refs_5_
  109.2 13.6 %shard_map.91 = bf16[1024,2048]{1,0:T(8,128)(2,1)} custom-call(s32[8]{0:T(128)S(1)} %broadcast_add_fusion.1.refs_0_, bf16[2,128,2048]{2,1,0:T(8,128)(2,1)S(1)} %get-tuple-element.59.refs_1_, bf16[2,128,2048]{2,1,0:T(8,128)(2,1)S(1)} %shard_map.89.refs_2_, bf16[2,128,2048]{2,1,0:T(8,128)(2,1)S(1)} %shard_map.90.refs_3_, ...), custom_call_target="tpu_custom_call", output_to_operand_aliasing={{}: (8, {})} | custom-call | flops 4600000000 | tf_op jit(solution)/shard_map/pallas_call | solution.py:515
  (5 shorter events, 0.0 us)
Async XLA Ops:
  0.6 7.6 %copy-start.5 = (s32[8,2]{0,1:T(2,128)S(1)}, s32[8,2]{0,1:T(2,128)}, u32[]{:S(2)}) copy-start(s32[8,2]{0,1:T(2,128)} %param.10) | copy-start | bytes 196
  0.6 7.6 %copy-start.6 = (s32[8,2]{0,1:T(2,128)S(1)}, s32[8,2]{0,1:T(2,128)}, u32[]{:S(2)}) copy-start(s32[8,2]{0,1:T(2,128)} %param.11) | copy-start | bytes 196
  0.7 7.6 %copy-start.3 = (s32[8]{0:T(128)S(1)}, s32[8]{0:T(128)}, u32[]{:S(2)}) copy-start(s32[8]{0:T(128)} %length_ref.1) | copy-start | bytes 100
  2.2 6.1 %collective-permute-start.1 = (bf16[256,256]{1,0:T(8,128)(2,1)}, bf16[256,256]{1,0:T(8,128)(2,1)S(1)}, u32[]{:S(2)}, u32[]{:S(2)}) collective-permute-start(bf16[256,256]{1,0:T(8,128)(2,1)} %shard_map.85), channel_id=1, source_target_pairs={{0,2},{4,0},{8,4},{12,8},{14,12},{10,14},{6,10},{2,6},{1,3},{5,1},... | collective-permute-start | bytes 393224 | tf_op jit(solution)/shard_map/ppermute | solution.py:634
  2.8 5.5 %collective-permute-start = (bf16[256,256]{1,0:T(8,128)(2,1)}, bf16[256,256]{1,0:T(8,128)(2,1)S(1)}, u32[]{:S(2)}, u32[]{:S(2)}) collective-permute-start(bf16[256,256]{1,0:T(8,128)(2,1)} %shard_map.85), channel_id=1, source_target_pairs={{0,4},{4,8},{8,12},{12,14},{14,10},{10,6},{6,2},{2,0},{1,5},{5,9},... | collective-permute-start | bytes 393224 | tf_op jit(solution)/shard_map/ppermute | solution.py:634
  6.1 18.8 %collective-permute-start.8 = (bf16[64,2048]{1,0:T(8,128)(2,1)}, bf16[64,2048]{1,0:T(8,128)(2,1)S(1)}, u32[]{:S(2)}, u32[]{:S(2)}) collective-permute-start(bf16[64,2048]{1,0:T(8,128)(2,1)} %get-tuple-element.52), channel_id=1, source_target_pairs={{0,2},{4,0},{8,4},{12,8},{14,12},{10,14},{6,10},{2,6},{1,3},{5,1},... | collective-permute-start | bytes 786440 | tf_op jit(solution)/shard_map/ppermute | solution.py:634
  6.7 18.2 %collective-permute-start.7 = (bf16[64,2048]{1,0:T(8,128)(2,1)}, bf16[64,2048]{1,0:T(8,128)(2,1)S(1)}, u32[]{:S(2)}, u32[]{:S(2)}) collective-permute-start(bf16[64,2048]{1,0:T(8,128)(2,1)} %get-tuple-element.52), channel_id=1, source_target_pairs={{0,4},{4,8},{8,12},{12,14},{14,10},{10,6},{6,2},{2,0},{1,5},{5,9},... | collective-permute-start | bytes 786440 | tf_op jit(solution)/shard_map/ppermute | solution.py:634
  8.3 16.7 %copy-start.4 = (bf16[64,2048]{1,0:T(8,128)(2,1)S(1)}, bf16[64,2048]{1,0:T(8,128)(2,1)}, u32[]{:S(2)}) copy-start(bf16[64,2048]{1,0:T(8,128)(2,1)} %get-tuple-element.56) | copy-start | bytes 786436
  8.3 29.4 %copy-start = (bf16[256,256]{1,0:T(8,128)(2,1)S(1)}, bf16[256,256]{1,0:T(8,128)(2,1)}, u32[]{:S(2)}) copy-start(bf16[256,256]{1,0:T(8,128)(2,1)} %refs_1_.1) | copy-start | bytes 393220
  8.3 29.4 %copy-start.1 = (bf16[256,256]{1,0:T(8,128)(2,1)S(1)}, bf16[256,256]{1,0:T(8,128)(2,1)}, u32[]{:S(2)}) copy-start(bf16[256,256]{1,0:T(8,128)(2,1)} %refs_2_.1) | copy-start | bytes 393220
  8.4 14.5 %collective-permute-start.2 = (bf16[256,256]{1,0:T(8,128)(2,1)S(1)}, bf16[256,256]{1,0:T(8,128)(2,1)S(1)}, u32[]{:S(2)}, u32[]{:S(2)}) collective-permute-start(bf16[256,256]{1,0:T(8,128)(2,1)S(1)} %collective-permute-done.refs_3_), channel_id=1, source_target_pairs={{0,4},{4,8},{8,12},{12,14},{14,10},{10,6},{6,2},{2,0},{1,5},{5,9},... | collective-permute-start | bytes 393224 | tf_op jit(solution)/shard_map/ppermute | solution.py:634
  9.5 13.4 %collective-permute-start.3 = (bf16[256,256]{1,0:T(8,128)(2,1)S(1)}, bf16[256,256]{1,0:T(8,128)(2,1)S(1)}, u32[]{:S(2)}, u32[]{:S(2)}) collective-permute-start(bf16[256,256]{1,0:T(8,128)(2,1)S(1)} %collective-permute-done.1.refs_4_), channel_id=1, source_target_pairs={{0,2},{4,0},{8,4},{12,8},{14,12},{10,14},{6,10},{2,6},{1,3},{5,1},... | collective-permute-start | bytes 393224 | tf_op jit(solution)/shard_map/ppermute | solution.py:634
  22.9 6.5 %collective-permute-start.4 = (bf16[256,256]{1,0:T(8,128)(2,1)S(1)}, bf16[256,256]{1,0:T(8,128)(2,1)S(1)}, u32[]{:S(2)}, u32[]{:S(2)}) collective-permute-start(bf16[256,256]{1,0:T(8,128)(2,1)S(1)} %collective-permute-done.2.refs_5_), channel_id=1, source_target_pairs={{0,4},{4,8},{8,12},{12,14},{14,10},{10,6},{6,2},{2,0},{1,5},{5,9},... | collective-permute-start | bytes 393224 | tf_op jit(solution)/shard_map/ppermute | solution.py:634
  22.9 6.5 %collective-permute-start.5 = (bf16[256,256]{1,0:T(8,128)(2,1)S(1)}, bf16[256,256]{1,0:T(8,128)(2,1)S(1)}, u32[]{:S(2)}, u32[]{:S(2)}) collective-permute-start(bf16[256,256]{1,0:T(8,128)(2,1)S(1)} %collective-permute-done.3.refs_6_), channel_id=1, source_target_pairs={{0,2},{4,0},{8,4},{12,8},{14,12},{10,14},{6,10},{2,6},{1,3},{5,1},... | collective-permute-start | bytes 393224 | tf_op jit(solution)/shard_map/ppermute | solution.py:634
  25.0 10.0 %collective-permute-start.10 = (bf16[64,2048]{1,0:T(8,128)(2,1)S(1)}, bf16[64,2048]{1,0:T(8,128)(2,1)S(1)}, u32[]{:S(2)}, u32[]{:S(2)}) collective-permute-start(bf16[64,2048]{1,0:T(8,128)(2,1)S(1)} %copy-done.4), channel_id=1, source_target_pairs={{0,2},{4,0},{8,4},{12,8},{14,12},{10,14},{6,10},{2,6},{1,3},{5,1},... | collective-permute-start | bytes 786440 | tf_op jit(solution)/shard_map/ppermute | solution.py:634
  25.0 10.0 %collective-permute-start.9 = (bf16[64,2048]{1,0:T(8,128)(2,1)S(1)}, bf16[64,2048]{1,0:T(8,128)(2,1)S(1)}, u32[]{:S(2)}, u32[]{:S(2)}) collective-permute-start(bf16[64,2048]{1,0:T(8,128)(2,1)S(1)} %copy-done.4), channel_id=1, source_target_pairs={{0,4},{4,8},{8,12},{12,14},{14,10},{10,6},{6,2},{2,0},{1,5},{5,9},... | collective-permute-start | bytes 786440 | tf_op jit(solution)/shard_map/ppermute | solution.py:634
  29.4 8.3 %collective-permute-start.6 = (bf16[256,256]{1,0:T(8,128)(2,1)S(1)}, bf16[256,256]{1,0:T(8,128)(2,1)S(1)}, u32[]{:S(2)}, u32[]{:S(2)}) collective-permute-start(bf16[256,256]{1,0:T(8,128)(2,1)S(1)} %collective-permute-done.4.refs_7_), channel_id=1, source_target_pairs={{0,4},{4,8},{8,12},{12,14},{14,10},{10,6},{6,2},{2,0},{1,5},{5,9},... | collective-permute-start | bytes 393224 | tf_op jit(solution)/shard_map/ppermute | solution.py:634
  30.9 32.1 %collective-permute-start.11 = (bf16[64,2048]{1,0:T(8,128)(2,1)S(1)}, bf16[64,2048]{1,0:T(8,128)(2,1)S(1)}, u32[]{:S(2)}, u32[]{:S(2)}) collective-permute-start(bf16[64,2048]{1,0:T(8,128)(2,1)S(1)} %collective-permute-done.7.refs_10_), channel_id=1, source_target_pairs={{0,4},{4,8},{8,12},{12,14},{14,10},{10,6},{6,2},{2,0},{1,5},{5,9},... | collective-permute-start | bytes 786440 | tf_op jit(solution)/shard_map/ppermute | solution.py:634
  30.9 32.0 %collective-permute-start.12 = (bf16[64,2048]{1,0:T(8,128)(2,1)S(1)}, bf16[64,2048]{1,0:T(8,128)(2,1)S(1)}, u32[]{:S(2)}, u32[]{:S(2)}) collective-permute-start(bf16[64,2048]{1,0:T(8,128)(2,1)S(1)} %collective-permute-done.8.refs_12_), channel_id=1, source_target_pairs={{0,2},{4,0},{8,4},{12,8},{14,12},{10,14},{6,10},{2,6},{1,3},{5,1},... | collective-permute-start | bytes 786440 | tf_op jit(solution)/shard_map/ppermute | solution.py:634
  35.0 30.0 %collective-permute-start.13 = (bf16[64,2048]{1,0:T(8,128)(2,1)S(1)}, bf16[64,2048]{1,0:T(8,128)(2,1)S(1)}, u32[]{:S(2)}, u32[]{:S(2)}) collective-permute-start(bf16[64,2048]{1,0:T(8,128)(2,1)S(1)} %collective-permute-done.9.refs_11_), channel_id=1, source_target_pairs={{0,4},{4,8},{8,12},{12,14},{14,10},{10,6},{6,2},{2,0},{1,5},{5,9},... | collective-permute-start | bytes 786440 | tf_op jit(solution)/shard_map/ppermute | solution.py:634
  36.5 28.5 %collective-permute-start.14 = (bf16[64,2048]{1,0:T(8,128)(2,1)S(1)}, bf16[64,2048]{1,0:T(8,128)(2,1)S(1)}, u32[]{:S(2)}, u32[]{:S(2)}) collective-permute-start(bf16[64,2048]{1,0:T(8,128)(2,1)S(1)} %collective-permute-done.10.refs_13_), channel_id=1, source_target_pairs={{0,2},{4,0},{8,4},{12,8},{14,12},{10,14},{6,10},{2,6},{1,3},{5,1},... | collective-permute-start | bytes 786440 | tf_op jit(solution)/shard_map/ppermute | solution.py:634
  37.7 1.2 copy-start.2
  62.9 21.6 %collective-permute-start.15 = (bf16[64,2048]{1,0:T(8,128)(2,1)S(1)}, bf16[64,2048]{1,0:T(8,128)(2,1)S(1)}, u32[]{:S(2)}, u32[]{:S(2)}) collective-permute-start(bf16[64,2048]{1,0:T(8,128)(2,1)S(1)} %collective-permute-done.11.refs_1_), channel_id=1, source_target_pairs={{0,4},{4,8},{8,12},{12,14},{14,10},{10,6},{6,2},{2,0},{1,5},{5,9},... | collective-permute-start | bytes 786440 | tf_op jit(solution)/shard_map/ppermute | solution.py:634
  63.0 21.6 %collective-permute-start.16 = (bf16[64,2048]{1,0:T(8,128)(2,1)S(1)}, bf16[64,2048]{1,0:T(8,128)(2,1)S(1)}, u32[]{:S(2)}, u32[]{:S(2)}) collective-permute-start(bf16[64,2048]{1,0:T(8,128)(2,1)S(1)} %collective-permute-done.12.refs_3_), channel_id=1, source_target_pairs={{0,2},{4,0},{8,4},{12,8},{14,12},{10,14},{6,10},{2,6},{1,3},{5,1},... | collective-permute-start | bytes 786440 | tf_op jit(solution)/shard_map/ppermute | solution.py:634
  65.0 19.6 %collective-permute-start.17 = (bf16[64,2048]{1,0:T(8,128)(2,1)S(1)}, bf16[64,2048]{1,0:T(8,128)(2,1)S(1)}, u32[]{:S(2)}, u32[]{:S(2)}) collective-permute-start(bf16[64,2048]{1,0:T(8,128)(2,1)S(1)} %collective-permute-done.13.refs_2_), channel_id=1, source_target_pairs={{0,4},{4,8},{8,12},{12,14},{14,10},{10,6},{6,2},{2,0},{1,5},{5,9},... | collective-permute-start | bytes 786440 | tf_op jit(solution)/shard_map/ppermute | solution.py:634
  65.1 19.6 %collective-permute-start.18 = (bf16[64,2048]{1,0:T(8,128)(2,1)S(1)}, bf16[64,2048]{1,0:T(8,128)(2,1)S(1)}, u32[]{:S(2)}, u32[]{:S(2)}) collective-permute-start(bf16[64,2048]{1,0:T(8,128)(2,1)S(1)} %collective-permute-done.14.refs_4_), channel_id=1, source_target_pairs={{0,2},{4,0},{8,4},{12,8},{14,12},{10,14},{6,10},{2,6},{1,3},{5,1},... | collective-permute-start | bytes 786440 | tf_op jit(solution)/shard_map/ppermute | solution.py:634
  84.6 24.6 %collective-permute-start.19 = (bf16[64,2048]{1,0:T(8,128)(2,1)S(1)}, bf16[64,2048]{1,0:T(8,128)(2,1)S(1)}, u32[]{:S(2)}, u32[]{:S(2)}) collective-permute-start(bf16[64,2048]{1,0:T(8,128)(2,1)S(1)} %collective-permute-done.15.refs_1_), channel_id=1, source_target_pairs={{0,4},{4,8},{8,12},{12,14},{14,10},{10,6},{6,2},{2,0},{1,5},{5,9},... | collective-permute-start | bytes 786440 | tf_op jit(solution)/shard_map/ppermute | solution.py:634
  84.7 24.5 %collective-permute-start.20 = (bf16[64,2048]{1,0:T(8,128)(2,1)S(1)}, bf16[64,2048]{1,0:T(8,128)(2,1)S(1)}, u32[]{:S(2)}, u32[]{:S(2)}) collective-permute-start(bf16[64,2048]{1,0:T(8,128)(2,1)S(1)} %collective-permute-done.18.refs_4_), channel_id=1, source_target_pairs={{0,2},{4,0},{8,4},{12,8},{14,12},{10,14},{6,10},{2,6},{1,3},{5,1},... | collective-permute-start | bytes 786440 | tf_op jit(solution)/shard_map/ppermute | solution.py:634
